TPU v7x, 512 devices: a whole 4x8x8 slice. The times are simulated.
512 devices in a mesh: ctx: 128 (over y, z, core), head: 4 (over x).
Axes of the slice: x: 4, y: 8, z: 8, core: 2. Of those that a mesh axis runs over, the one named last changes fastest.
Arguments:
- queries: bfloat16 [1024, 36864], P('ctx', 'head'), may hold values from -24 to 24
- grad_out: bfloat16 [1024, 32768], P('ctx', 'head'), may hold values from -24 to 24
- latent: bfloat16 [512, 64, 576], P('ctx'), may hold values from -6 to 6
- selected: int32 [128, 32], P('ctx'), may hold values from -1 to 511, as said below
Outputs:
- query_grad: bfloat16 [1024, 36864], P('ctx', 'head')
- latent_grad: bfloat16 [512, 64, 576], P('ctx', None, 'head')
Inputs may be any that keep to these rules, and one draw needn't show every extreme that they name: `selected`: entry 0 of row c is c * 4 + 3. Each other entry is -1 or a block of a lower index of ctx (blocks d * 4 .. d * 4 + 3 belong to index d), no two entries of a row on the same index; row c has min(32, c + 1) entries that are not -1, and for c >= 1 one of them is a block of index 0.
All inputs are finite; a program needn't handle non-finite values.
Results may differ from a plain program's by a relative error of at most 0.015.
Values may be sent and summed in bfloat16 or wider, within the bound.
A program may use at most 128 MiB of HBM per device.

v0:
```python
import jax
import jax.numpy as jnp
from jax import lax
from jax.sharding import PartitionSpec as P

softmax_scale = 192.0 ** (-0.5)


def local(queries, grad_out, latent, selected):
    blocks, block_rows, lat_width = latent.shape
    query_count = queries.shape[0]
    heads_here = queries.shape[1] // lat_width
    value_width = grad_out.shape[1] // heads_here
    slots = selected.shape[1]
    ctx_count = lax.axis_size("ctx")
    head_count = lax.axis_size("head")
    quarter = lat_width // head_count
    position = lax.axis_index("ctx")
    requests = lax.all_gather(selected, "ctx", axis=0, tiled=True)
    wanted = selected[0]
    local_index = requests - position * blocks
    hits = (local_index >= 0) & (local_index < blocks)
    send_index = jnp.sum(jnp.where(hits, local_index, 0), axis=1)
    send_live = jnp.any(hits, axis=1)
    owners = jnp.where(wanted >= 0, wanted // blocks, 0)
    share = lax.dynamic_slice_in_dim(latent, lax.axis_index("head") * quarter, quarter, 2)
    outgoing = jnp.where(send_live[:, None, None], share[send_index], jnp.zeros((), jnp.bfloat16))
    arrived = lax.all_to_all(
        outgoing.reshape(ctx_count, block_rows * quarter),
        "ctx",
        split_axis=0,
        concat_axis=0,
        tiled=True,
    )
    mine = arrived[owners].reshape(slots, block_rows, quarter)
    tiles = lax.all_gather(mine, "head", axis=2, tiled=True)
    key_count = slots * block_rows
    row_count = query_count * heads_here
    keys = tiles.reshape(key_count, lat_width)
    rows = queries.reshape(row_count, lat_width)
    out_rows = grad_out.reshape(row_count, value_width)
    own = position * blocks + blocks - 1
    key_slot = jnp.arange(key_count, dtype=jnp.int32) // block_rows
    key_pos = jnp.arange(key_count, dtype=jnp.int32) % block_rows
    query_pos = block_rows - query_count + jnp.arange(row_count, dtype=jnp.int32) // heads_here
    slot_ids = wanted[key_slot]
    seen = (slot_ids[None, :] >= 0) & (
        (slot_ids[None, :] != own) | (key_pos[None, :] <= query_pos[:, None])
    )
    scores = softmax_scale * jnp.dot(rows, keys.T, preferred_element_type=jnp.float32)
    top = jnp.max(jnp.where(seen, scores, -jnp.inf), axis=1, keepdims=True)
    weights = jnp.where(seen, jnp.exp(scores - top), 0.0)
    probs = weights / jnp.sum(weights, axis=1, keepdims=True)
    probs16 = probs.astype(jnp.bfloat16)
    values = keys[:, :value_width]
    dprobs = jnp.dot(out_rows, values.T, preferred_element_type=jnp.float32)
    delta = jnp.sum(probs * dprobs, axis=1, keepdims=True)
    dscores16 = (probs * (dprobs - delta)).astype(jnp.bfloat16)
    query_grad = (
        softmax_scale * jnp.dot(dscores16, keys, preferred_element_type=jnp.float32)
    ).astype(jnp.bfloat16)
    dkeys = softmax_scale * jnp.dot(dscores16.T, rows, preferred_element_type=jnp.float32)
    dvalues = jnp.dot(probs16.T, out_rows, preferred_element_type=jnp.float32)
    key_part = dkeys.at[:, :value_width].add(dvalues).reshape(slots, block_rows, lat_width)
    summed = lax.psum_scatter(
        key_part.astype(jnp.bfloat16), "head", scatter_dimension=2, tiled=True
    ).astype(jnp.float32)
    live_slot = (wanted >= 0)[:, None]
    flat_terms = jnp.where(live_slot, summed.reshape(slots, block_rows * quarter), 0.0)
    packed = jnp.zeros((ctx_count, block_rows * quarter), jnp.float32).at[owners].add(flat_terms)
    back = lax.all_to_all(
        packed.astype(jnp.bfloat16), "ctx", split_axis=0, concat_axis=0, tiled=True
    ).astype(packed.dtype)
    arriving = jnp.where(send_live[:, None], back, 0.0)
    latent_grad = (
        jnp.zeros((blocks, block_rows * quarter), jnp.float32).at[send_index].add(arriving)
    )
    latent_grad = latent_grad.reshape(blocks, block_rows, quarter).astype(jnp.bfloat16)
    return (query_grad.reshape(query_count, heads_here * lat_width), latent_grad)


def solution(mesh):
    placed = (P("ctx", "head"), P("ctx", "head"), P("ctx", None, None), P("ctx", None))
    return jax.shard_map(
        local,
        mesh=mesh,
        in_specs=placed,
        out_specs=(P("ctx", "head"), P("ctx", None, "head")),
        check_vma=False,
    )
```

profile of v0, /device:TPU:1, one launch (start us, length us, event | category | flops | bytes accessed | tf_op | source)
XLA Modules:
  0.0 418.8 jit_solution(5941953481651552806)
XLA Ops:
  7.2 52.0 %all-gather = s32[128,1,32]{2,1,0:T(1,128)S(1)} all-gather(s32[1,1,32]{2,1,0:T(1,128)} %bitcast.93), channel_id=1, replica_groups=mesh['ctx'=128,'head'=4] {'ctx'}, dimensions={0}, use_global_device_ids=true | all-gather | bytes 16512 | tf_op jit(solution)/shard_map/all_gather | solution.py:19
  62.4 6.1 %copy.19 = bf16[128,64,144]{0,2,1:T(8,128)(2,1)S(1)} copy(bf16[128,64,144]{2,1,0:T(8,128)(2,1)} %gather_fusion) | data formatting | bytes 4718592 | tf_op jit(solution)/shard_map/gather | solution.py:27
  70.5 3.1 reduce.58
  76.2 4.7 %reshape.537 = bf16[128,2,4608]{2,1,0:T(2,128)(2,1)} reshape(bf16[128,9216]{1,0:T(8,128)(2,1)} %copy.36) | data formatting | bytes 4718592
  80.9 9.2 %all-to-all-start = ((bf16[128,2,4608]{2,1,0:T(2,128)(2,1)}), bf16[128,2,4608]{2,1,0:T(2,128)(2,1)S(1)}, u32[]{:S(2)}, u32[]{:S(2)}) async-start(bf16[128,2,4608]{2,1,0:T(2,128)(2,1)} %reshape.537), calls=%async_computation | async-start | bytes 4718592 | tf_op jit(solution)/shard_map/all_to_all | solution.py:28
  90.1 57.4 %all-to-all-done = bf16[128,2,4608]{2,1,0:T(2,128)(2,1)S(1)} async-done(((bf16[128,2,4608]{2,1,0:T(2,128)(2,1)}), bf16[128,2,4608]{2,1,0:T(2,128)(2,1)S(1)}, u32[]{:S(2)}, u32[]{:S(2)}) %all-to-all-start) | async-done | bytes 2359328 | tf_op jit(solution)/shard_map/all_to_all | solution.py:28
  147.6 6.7 %reshape.538 = bf16[128,1,9216]{2,1,0:T(2,128)(2,1)} reshape(bf16[128,2,4608]{2,1,0:T(2,128)(2,1)S(1)} %all-to-all-done) | data formatting | bytes 4718592
  154.3 3.1 copy.35
  166.0 4.4 %compare_select_fusion.1 = s32[2048,1]{0,1:T(1,128)S(1)} fusion(s32[]{:T(128)} %bitcast.25, s32[]{:T(128)} %bitcast.26, s32[]{:T(128)} %bitcast.27, s32[]{:T(128)} %bitcast.28, s32[]{:T(128)} %bitcast.29, s32[]{:T(128)} %bitcast.31, s32[]{:T(128)} %bitcast.30), kind=kLoop, calls=%fused_computation.66 | loop fusion | flops 47104 | bytes 8220 | tf_op jit(solution)/shard_map/gather | solution.py:46
  170.3 15.6 %broadcast_compare_fusion = (pred[2048]{0:T(1024)(128)(4,1)S(1)}, s32[2048]{0:T(1024)S(1)}) fusion(pred[2048]{0:T(1024)(128)(4,1)S(1)} %compare_reduce_fusion, pred[2048]{0:T(1024)(128)(4,1)S(1)} %compare_reduce_fusion.1, pred[2048]{0:T(1024)(128)(4,1)S(1)} %compare_reduce_fusion.2, pred[2048]{0:T(1024)(128)(4,1)S(1)} %compare_reduce_fusion.3, ...), kind=kLoop, calls=%fused_computation.84 | loop fusion | flops 53248 | bytes 69732 | tf_op jit(solution)/shard_map/ge | solution.py:47
  185.9 29.5 %all-gather.3.cloned.1.call-done = bf16[32,64,576]{1,0,2:T(8,128)(2,1)} async-done(((bf16[32,64,144]{1,0,2:T(8,128)(2,1)}), bf16[32,64,576]{1,0,2:T(8,128)(2,1)}) %all-gather.3.cloned.1.call-update) | async-done | bytes 2359312 | tf_op jit(solution)/shard_map/all_gather | solution.py:36
  215.4 6.8 %copy.22 = bf16[32,64,576]{2,1,0:T(8,128)(2,1)S(1)} copy(bf16[32,64,576]{1,0,2:T(8,128)(2,1)} %all-gather.3.cloned.1.call-done) | data formatting | bytes 4718592 | tf_op jit(solution)/shard_map/all_gather | solution.py:36
  232.8 3.1 copy.24
  235.9 7.9 %copy.27 = bf16[32,64,576]{1,0,2:T(8,128)(2,1)} copy(bf16[32,64,576]{2,1,0:T(8,128)(2,1)S(1)} %bitcast.85) | data formatting | bytes 4718592
  243.8 7.7 %reshape.506 = bf16[576,2048]{1,0:T(8,128)(2,1)} reshape(bf16[576,32,64]{2,1,0:T(8,128)(2,1)} %bitcast.84) | data formatting | bytes 4718592
  251.4 37.8 %reduce-scatter.4.cloned.1.call-done = bf16[144,2048]{1,0:T(8,128)(2,1)} async-done(((bf16[576,2048]{1,0:T(8,128)(2,1)}), bf16[144,2048]{1,0:T(8,128)(2,1)}) %reduce-scatter.4.cloned.1.call-update) | async-done | bytes 589840
  294.7 4.4 %scatter_custom_fusion = f32[128,9216]{1,0:T(8,128)} fusion(s32[32]{0:T(128)S(1)} %fusion.24, f32[]{:T(128)} %constant.129.clone.1, f32[32,9216]{1,0:T(8,128)S(1)} %reshape.284, pred[32]{0:T(512)(128)(4,1)S(1)} %compare_bitcast_fusion), kind=kCustom, calls=%fused_computation.18 | custom fusion | flops 589824 | bytes 5899776 | tf_op jit(solution)/shard_map/scatter-add | solution.py:70
  301.7 3.1 reduce.59
  304.8 4.7 %reshape.539 = bf16[128,2,4608]{2,1,0:T(2,128)(2,1)} reshape(bf16[128,9216]{1,0:T(8,128)(2,1)} %reduce.59) | data formatting | bytes 4718592
  309.5 14.2 %all-to-all-start.1 = ((bf16[128,2,4608]{2,1,0:T(2,128)(2,1)}), bf16[128,2,4608]{2,1,0:T(2,128)(2,1)S(1)}, u32[]{:S(2)}, u32[]{:S(2)}) async-start(bf16[128,2,4608]{2,1,0:T(2,128)(2,1)} %reshape.539), calls=%async_computation.1 | async-start | bytes 4718592 | tf_op jit(solution)/shard_map/all_to_all | solution.py:71
  323.7 3.8 fusion.11
  328.5 52.7 %all-to-all-done.1 = bf16[128,2,4608]{2,1,0:T(2,128)(2,1)S(1)} async-done(((bf16[128,2,4608]{2,1,0:T(2,128)(2,1)}), bf16[128,2,4608]{2,1,0:T(2,128)(2,1)S(1)}, u32[]{:S(2)}, u32[]{:S(2)}) %all-to-all-start.1) | async-done | bytes 2359328 | tf_op jit(solution)/shard_map/all_to_all | solution.py:71
  381.2 6.7 %reshape.540 = bf16[128,1,9216]{2,1,0:T(2,128)(2,1)} reshape(bf16[128,2,4608]{2,1,0:T(2,128)(2,1)S(1)} %all-to-all-done.1) | data formatting | bytes 4718592
  388.0 22.8 %scatter_custom_fusion.1 = f32[4,9216]{1,0:T(4,128)S(1)} fusion(s32[128]{0:T(128)S(1)} %fusion.23, bf16[128,1,9216]{2,1,0:T(2,128)(2,1)} %reshape.540, f32[]{:T(128)} %constant.129.clone.1, pred[128]{0:T(512)(128)(4,1)S(1)} %fusion.18), kind=kCustom, calls=%fused_computation.6 | custom fusion | flops 3538944 | bytes 4867584 | tf_op jit(solution)/shard_map/scatter-add | solution.py:76
  (83 shorter events, 36.7 us)
Async XLA Ops:
  7.2 52.3 %copy-start = (bf16[4,64,576]{2,1,0:T(8,128)(2,1)S(1)}, bf16[4,64,576]{2,1,0:T(8,128)(2,1)}, u32[]{:S(2)}) copy-start(bf16[4,64,576]{2,1,0:T(8,128)(2,1)} %param.8) | copy-start | bytes 884740
  80.9 9.3 %copy-start.4 = (s32[1,32]{1,0:T(1,128)S(1)}, s32[1,32]{1,0:T(1,128)}, u32[]{:S(2)}) copy-start(s32[1,32]{1,0:T(1,128)} %param.9) | copy-start | bytes 388
  80.9 66.7 %all-to-all-start = ((bf16[128,2,4608]{2,1,0:T(2,128)(2,1)}), bf16[128,2,4608]{2,1,0:T(2,128)(2,1)S(1)}, u32[]{:S(2)}, u32[]{:S(2)}) async-start(bf16[128,2,4608]{2,1,0:T(2,128)(2,1)} %reshape.537), calls=%async_computation | async-start | bytes 4718592 | tf_op jit(solution)/shard_map/all_to_all | solution.py:28
  90.1 125.3 %all-gather.3.cloned.1.call-start = ((), (), s32[]{:S(2)}) async-start(), calls=%async_computation.3 | async-start | bytes 5898240 | tf_op jit(solution)/shard_map/all_gather | solution.py:36
  158.3 3.9 copy-start.5
  158.3 4.0 copy-start.6
  162.1 127.1 %reduce-scatter.4.cloned.1.call-start = ((), (), s32[]{:S(2)}) async-start(), calls=%async_computation.4 | async-start | bytes 2949120
  222.1 3.7 copy-start.2
  223.2 4.9 %copy-start.3 = (f32[128,2048]{0,1:T(8,128)}, f32[128,2048]{0,1:T(8,128)S(1)}, u32[]{:S(2)}) copy-start(f32[128,2048]{0,1:T(8,128)S(1)} %get-tuple-element.49) | copy-start | bytes 3145732
  225.8 1.0 copy-start.7
  309.5 71.8 %all-to-all-start.1 = ((bf16[128,2,4608]{2,1,0:T(2,128)(2,1)}), bf16[128,2,4608]{2,1,0:T(2,128)(2,1)S(1)}, u32[]{:S(2)}, u32[]{:S(2)}) async-start(bf16[128,2,4608]{2,1,0:T(2,128)(2,1)} %reshape.539), calls=%async_computation.1 | async-start | bytes 4718592 | tf_op jit(solution)/shard_map/all_to_all | solution.py:71
  381.2 30.5 %copy-start.1 = (bf16[4,64,576]{2,1,0:T(8,128)(2,1)S(1)}, bf16[4,64,576]{2,1,0:T(8,128)(2,1)}, u32[]{:S(2)}) copy-start(bf16[4,64,576]{2,1,0:T(8,128)(2,1)} %param.8) | copy-start | bytes 884740
Sparse Core Ops, SparseCore 0:
  162.2 53.0 all-gather.2
  251.6 37.6 reduce-scatter.3
where the time goes:
time: 427 us; the launch traced here: 419 us
  waiting for transfers between devices  177 us (41%)
  local copies, waits for them, and re-layouts  77.9 us (18%)
  other arithmetic  63.2 us (15%)
  blocking collectives  52 us (12%)
  starting transfers between devices  23.5 us (6%)
  between operations  14.6 us (3%)
  matrix products  10 us (2%)
    all_to_all x1, waiting for transfers between devices, local(): lax.all_to_all(outgoing.reshape(ctx_count, block_rows * quarter), 'ctx',...  57.4 us
    all_to_all x1, waiting for transfers between devices, local(): lax.all_to_all(packed.astype(jnp.bfloat16), 'ctx', split_axis=0, concat_a...  52.7 us
    all_gather x1, blocking collectives, local(): requests = lax.all_gather(selected, 'ctx', axis=0, tiled=True)  52 us
    unnamed x26, local copies, waits for them, and re-layouts  48.6 us
    unnamed x3, waiting for transfers between devices  37.9 us
    all_gather x1, waiting for transfers between devices, local(): tiles = lax.all_gather(mine, 'head', axis=2, tiled=True)  29.5 us
    scatter-add x1, other arithmetic, local(): jnp.zeros((blocks, block_rows * quarter), jnp.float32).at[send_index]  22.8 us
    ge x1, other arithmetic, local(): slot_ids[None, :] >= 0  15.6 us
  transfers between devices with their start and end apart: 4, of which 4 were waited for; matrix products, arithmetic and copies ran while one was open for 7% of the time, Pallas kernels for 0%

commit v1 on v0

v1 whole, which is shorter than its diff:
```python
import functools

import jax
import jax.numpy as jnp
from jax import lax
from jax.experimental import pallas as pl
from jax.experimental.pallas import tpu as pltpu
from jax.sharding import PartitionSpec as P

MESH = pl.DeviceIdType.MESH
BF16 = jnp.bfloat16
F32 = jnp.float32
SCALE = 192.0 ** (-0.5)

NY, NZ, NK, NX = 8, 8, 2, 4
RING = 8
BLK, LAT, VDIM = 64, 576, 512
WIDE = 640
ROWS = 288
HALF = 144
QBLK, HEADS_HERE = 8, 16
QR = QBLK * HEADS_HERE
ALLR = QR * NX
SLOTS = 32
CHUNK = 4
CK = CHUNK * BLK
NEG = -1e30
VMEM_LIMIT = 56 * 1024 * 1024

OFFS = (0, -1, 1, -2, 2, -3, 3, -4)
UP = (4, 4, 4, 4, 3, 3, 3, 3)
DOWN = (3, 3, 3, 3, 4, 4, 4, 4)


def where_am_i():
    ctx = lax.axis_index("ctx")
    x = lax.axis_index("head")
    core = lax.rem(ctx, NK)
    chip = ctx // NK
    return lax.rem(chip, NZ), chip // NZ, core, x


def ctx_of(y, z, core):
    return (y * NZ + z) * NK + core


def wrap(v, n):
    return lax.rem(v + 2 * n, n)


def place(half, first, second):
    return second * NZ + first if half == 0 else first * NZ + second


def neighbour(half, ring, step, y, z, core, x):
    along_z = (half == 0) == (ring == 0)
    if along_z:
        return (ctx_of(y, wrap(z + step, NZ), core), x)
    return (ctx_of(wrap(y + step, NY), z, core), x)


def gather_plan():
    plan = []
    for t in range(4):
        plan.append((t, 0, 1, t, 0))
        if t < 3:
            plan.append((t, 0, -1, t, 0))
    for q, off in enumerate(OFFS):
        for s in range(UP[q]):
            plan.append((s + abs(off), 1, 1, s, q))
        for s in range(DOWN[q]):
            plan.append((s + abs(off), 1, -1, s, q))
    return sorted(plan, key=lambda e: (e[0], e[1], -e[3], e[4], -e[2]))


def labels():
    names = {}
    for wave, ring, way, s, q in gather_plan():
        names[(ring, way, s + 1, q)] = len(names)
    return names


LABELS = labels()
NLAB = len(LABELS)


def enter(peers):
    barrier = pltpu.get_barrier_semaphore()
    for peer in peers:
        pl.semaphore_signal(barrier, inc=1, device_id=peer, device_id_type=MESH)
    pl.semaphore_wait(barrier, len(peers))


def ring_peers(y, z, core, x):
    return [neighbour(0, ring, step, y, z, core, x) for ring in (0, 1) for step in (1, -1)]


def group_peers(y, z, core, x):
    me = ctx_of(y, z, core)
    sibling = ctx_of(y, z, 1 - core)
    far = [(me, wrap(x + d, NX)) for d in (1, 2, 3)]
    across = [(sibling, wrap(x + d, NX)) for d in (0, 1, 2, 3)]
    return far, across


def pack_block(block):
    parts = [block[:, 128 * g : 128 * g + 128] for g in range(4)]
    return parts, block[:, VDIM:]


def gather_kernel(
    lat_ref, q_ref, g_ref, sel_ref,
    keys_out, q_out, g_out, sel_out,
    block, pack, qrow, grow, load_sem, local_sem, send_sem, recv_sem, gsend, grecv,
):
    z, y, core, x = where_am_i()
    chip = y * NZ + z
    load = pltpu.make_async_copy(lat_ref.at[x], block, load_sem)
    load.start()
    far, across = group_peers(y, z, core, x)
    enter(ring_peers(y, z, core, x) + far + across[:1])
    load.wait()
    wide = block[...].astype(F32)
    for g in range(4):
        pack[64 * g : 64 * g + 64, :] = block[:, 128 * g : 128 * g + 128]
    tail = jnp.concatenate([wide[:, VDIM:], jnp.zeros((BLK, 64), F32)], axis=1)
    pack[256:288, :] = (tail[:32] + pltpu.roll(tail[32:], 64, axis=1)).astype(BF16)
    keep = pltpu.make_async_copy(pack, keys_out.at[chip], local_sem.at[0])
    keep.start()

    first = {0: z, 1: y}
    second = {0: y, 1: z}
    sends = []
    arrived = set()

    def part(half):
        return pl.ds(HALF * half, HALF)

    def arrival(half, label):
        if (half, label) in arrived:
            return
        arrived.add((half, label))
        pltpu.make_async_copy(
            keys_out.at[chip, part(half)], keys_out.at[chip, part(half)],
            recv_sem.at[half * NLAB + LABELS[label]],
        ).wait()

    def send(half, ring, way, s, q):
        if ring == 0:
            off, along = -way * s, 0
            if s > 0:
                arrival(half, (0, way, s, 0))
        else:
            off, along = OFFS[q], -way * s
            if s > 0:
                arrival(half, (1, way, s, q))
            elif off != 0:
                arrival(half, (0, 1 if off < 0 else -1, abs(off), 0))
        spot = place(half, wrap(first[half] + off, RING), wrap(second[half] + along, RING))
        own = off == 0 and along == 0
        src = pack.at[part(half)] if own else keys_out.at[spot, part(half)]
        number = half * NLAB + LABELS[(ring, way, s + 1, q)]
        copy = pltpu.make_async_remote_copy(
            src_ref=src,
            dst_ref=keys_out.at[spot, part(half)],
            send_sem=send_sem.at[number],
            recv_sem=recv_sem.at[number],
            device_id=neighbour(half, ring, way, y, z, core, x),
            device_id_type=MESH,
        )
        copy.start()
        sends.append(copy)

    plan = gather_plan()
    waves = max(e[0] for e in plan) + 1

    def group_copy(src, out, kind, slot_core, slot_x, peer, number):
        copy = pltpu.make_async_remote_copy(
            src_ref=src,
            dst_ref=out.at[slot_core, slot_x] if kind != 2 else out.at[slot_core],
            send_sem=gsend.at[number],
            recv_sem=grecv.at[number],
            device_id=peer,
            device_id_type=MESH,
        )
        copy.start()
        sends.append(copy)

    group_number = {}

    def number_of(kind, hop):
        return group_number.setdefault((kind, hop), len(group_number))

    def group_arrival(kind, hop):
        ref = (q_out.at[0, 0], g_out.at[0, 0], sel_out.at[0])[kind]
        pltpu.make_async_copy(ref, ref, grecv.at[number_of(kind, hop)]).wait()

    for wave in range(waves):
        for entry in plan:
            if entry[0] == wave:
                for half in (0, 1):
                    send(half, *entry[1:])
        if wave == 0:
            group_copy(sel_ref, sel_out, 2, core, 0, across[0], number_of(2, 0))
            keep_sel = pltpu.make_async_copy(sel_ref, sel_out.at[core], local_sem.at[1])
            keep_sel.start()
            for pair in range(HEADS_HERE // 2):
                both = q_ref[:, 2 * LAT * pair : 2 * LAT * (pair + 1)].astype(F32)
                lane = lax.broadcasted_iota(jnp.int32, (QBLK, WIDE), 1)
                one = jnp.where(lane < LAT, both[:, :WIDE], 0.0)
                two = jnp.where(lane < LAT, pltpu.roll(both[:, VDIM:], WIDE - 64, axis=1), 0.0)
                qrow[16 * pair : 16 * pair + 16, :] = jnp.concatenate([one, two], axis=0).astype(BF16)
                one = g_ref[:, 2 * VDIM * pair : 2 * VDIM * pair + VDIM].astype(F32)
                two = g_ref[:, 2 * VDIM * pair + VDIM : 2 * VDIM * (pair + 1)].astype(F32)
                grow[16 * pair : 16 * pair + 16, :] = jnp.concatenate([one, two], axis=0).astype(BF16)
            for d in range(3):
                group_copy(qrow, q_out, 0, core, x, far[d], number_of(0, 3 - d))
                group_copy(grow, g_out, 1, core, x, far[d], number_of(1, 3 - d))
            group_copy(qrow, q_out, 0, core, x, across[0], number_of(0, 4))
            group_copy(grow, g_out, 1, core, x, across[0], number_of(1, 4))
            keep_q = pltpu.make_async_copy(qrow, q_out.at[core, x], local_sem.at[2])
            keep_q.start()
            keep_g = pltpu.make_async_copy(grow, g_out.at[core, x], local_sem.at[3])
            keep_g.start()
        if wave == 5:
            for d in (1, 3, 2):
                src_x = wrap(x + d, NX)
                group_arrival(0, d)
                group_copy(q_out.at[core, src_x], q_out, 0, core, src_x, across[0], number_of(0, 4 + d))
                group_arrival(1, d)
                group_copy(g_out.at[core, src_x], g_out, 1, core, src_x, across[0], number_of(1, 4 + d))

    for half in (0, 1):
        for label in LABELS:
            arrival(half, label)
    for kind in (0, 1):
        for hop in (4, 5, 6, 7):
            group_arrival(kind, hop)
    group_arrival(2, 0)
    for copy in sends:
        copy.wait_send()
    keep.wait()
    keep_sel.wait()
    keep_q.wait()
    keep_g.wait()


def gather_all(latent, queries, grad_out, selected):
    any_spec = pl.BlockSpec(memory_space=pl.ANY)
    vmem = pl.BlockSpec(memory_space=pltpu.VMEM)
    return pl.pallas_call(
        gather_kernel,
        out_shape=(
            jax.ShapeDtypeStruct((NY * NZ, ROWS, 128), BF16),
            jax.ShapeDtypeStruct((NK, NX, QR, WIDE), BF16),
            jax.ShapeDtypeStruct((NK, NX, QR, VDIM), BF16),
            jax.ShapeDtypeStruct((NK, 1, SLOTS), jnp.int32),
        ),
        in_specs=[any_spec, vmem, vmem, any_spec],
        out_specs=(any_spec, any_spec, any_spec, any_spec),
        scratch_shapes=[
            pltpu.VMEM((BLK, LAT), BF16),
            pltpu.VMEM((ROWS, 128), BF16),
            pltpu.VMEM((QR, WIDE), BF16),
            pltpu.VMEM((QR, VDIM), BF16),
            pltpu.SemaphoreType.DMA(()),
            pltpu.SemaphoreType.DMA((4,)),
            pltpu.SemaphoreType.DMA((2 * NLAB,)),
            pltpu.SemaphoreType.DMA((2 * NLAB,)),
            pltpu.SemaphoreType.DMA((15,)),
            pltpu.SemaphoreType.DMA((15,)),
        ],
        compiler_params=pltpu.CompilerParams(
            collective_id=0, has_side_effects=True, vmem_limit_bytes=VMEM_LIMIT
        ),
        cost_estimate=pl.CostEstimate(flops=0, bytes_accessed=10_000_000, transcendentals=0),
        name="gather_keys",
    )(latent, queries, grad_out, selected)


def list_slots(sel_ref, spots, owns, query_block, kind, own_id):
    def look(j, n):
        block_id = sel_ref[query_block, 0, j]
        mine = (block_id >= 0) & (lax.rem(block_id, 8) == kind)
        spots[n] = jnp.where(mine, block_id // 8, 0)
        owns[n] = jnp.where(mine & (block_id == own_id), 1, 0)
        return n + mine.astype(jnp.int32)

    count = lax.fori_loop(0, SLOTS, look, jnp.int32(0))
    for extra in range(CHUNK):
        spots[count + extra] = 0
        owns[count + extra] = 0
    return count


def load_chunk(chunk, spots, keys_ref, landed, kbuf, sem, slot):
    for i in range(CHUNK):
        pltpu.make_async_copy(
            keys_ref.at[spots[chunk * CHUNK + i]], landed.at[slot, i], sem.at[slot, i]
        ).start()


def take_chunk(keys_ref, landed, kbuf, sem, slot):
    lane = lax.broadcasted_iota(jnp.int32, (32, 128), 1)
    for i in range(CHUNK):
        pltpu.make_async_copy(keys_ref.at[0], landed.at[slot, i], sem.at[slot, i]).wait()
        for g in range(4):
            kbuf[64 * i : 64 * i + 64, 128 * g : 128 * g + 128] = landed[slot, i, 64 * g : 64 * g + 64, :]
        tail = landed[slot, i, 256:288, :].astype(F32)
        kbuf[64 * i : 64 * i + 32, VDIM:] = jnp.where(lane < 64, tail, 0.0).astype(BF16)
        kbuf[64 * i + 32 : 64 * i + 64, VDIM:] = jnp.where(
            lane < 64, pltpu.roll(tail, 64, axis=1), 0.0
        ).astype(BF16)


def seen_of(chunk, owns, count):
    row = lax.broadcasted_iota(jnp.int32, (BLK, ALLR), 0)
    col = lax.broadcasted_iota(jnp.int32, (BLK, ALLR), 1)
    limit = BLK - QBLK + lax.rem(col, QBLK)
    parts = []
    for i in range(CHUNK):
        slot = chunk * CHUNK + i
        top = jnp.where(slot < count, jnp.where(owns[slot] == 1, limit, BLK), -1)
        parts.append(row <= top)
    return jnp.concatenate(parts, axis=0)


def nt(a, b):
    return lax.dot_general(a, b, (((1,), (1,)), ((), ())), preferred_element_type=F32)


def tn(a, b):
    return lax.dot_general(a, b, (((0,), (0,)), ((), ())), preferred_element_type=F32)


def nn(a, b):
    return lax.dot_general(a, b, (((1,), (0,)), ((), ())), preferred_element_type=F32)


def stats_kernel(sel_ref, keys_ref, q_ref, g_ref, stats_ref, landed, kbuf, spots, owns, sem):
    z, y, core, x = where_am_i()
    chip = y * NZ + z
    for qb in range(NK):
        count = list_slots(sel_ref, spots, owns, qb, 4 * core + x, (chip * NK + qb) * 4 + 3)
        chunks = (count + CHUNK - 1) // CHUNK

        @pl.when(chunks > 0)
        def _():
            load_chunk(0, spots, keys_ref, landed, kbuf, sem, 0)

        def step(chunk, carry):
            top, total, delta = carry
            slot = lax.rem(chunk, 2)

            @pl.when(chunk + 1 < chunks)
            def _():
                load_chunk(chunk + 1, spots, keys_ref, landed, kbuf, sem, 1 - slot)

            take_chunk(keys_ref, landed, kbuf, sem, slot)
            seen = seen_of(chunk, owns, count)
            scores = SCALE * nt(kbuf[...], q_ref[qb])
            dprobs = nt(kbuf[:, :VDIM], g_ref[qb])
            scores = jnp.where(seen, scores, NEG)
            new_top = jnp.maximum(top, jnp.max(scores, axis=0, keepdims=True))
            weights = jnp.where(seen, jnp.exp(scores - new_top), 0.0)
            shrink = jnp.exp(top - new_top)
            total = total * shrink + jnp.sum(weights, axis=0, keepdims=True)
            delta = delta * shrink + jnp.sum(weights * dprobs, axis=0, keepdims=True)
            return new_top, total, delta

        zero = jnp.zeros((1, ALLR), F32)
        top, total, delta = lax.fori_loop(0, chunks, step, (zero + NEG, zero, zero))
        stats_ref[qb] = jnp.concatenate([top, total, delta, jnp.zeros((5, ALLR), F32)], axis=0)


def stats_of(sel, keys, queries, grad_out):
    vmem = pl.BlockSpec(memory_space=pltpu.VMEM)
    return pl.pallas_call(
        stats_kernel,
        out_shape=jax.ShapeDtypeStruct((NK, 8, ALLR), F32),
        in_specs=[
            pl.BlockSpec(memory_space=pltpu.SMEM),
            pl.BlockSpec(memory_space=pl.ANY),
            vmem,
            vmem,
        ],
        out_specs=vmem,
        scratch_shapes=[
            pltpu.VMEM((2, CHUNK, ROWS, 128), BF16),
            pltpu.VMEM((CK, WIDE), BF16),
            pltpu.SMEM((SLOTS + CHUNK,), jnp.int32),
            pltpu.SMEM((SLOTS + CHUNK,), jnp.int32),
            pltpu.SemaphoreType.DMA((2, CHUNK)),
        ],
        compiler_params=pltpu.CompilerParams(vmem_limit_bytes=VMEM_LIMIT),
        name="local_stats",
    )(sel, keys, queries, grad_out)


def share_kernel(mine, out, send_sem, recv_sem, local_sem):
    z, y, core, x = where_am_i()
    far, across = group_peers(y, z, core, x)
    enter(far + across)
    slot = x * NK + core
    keep = pltpu.make_async_copy(mine, out.at[slot], local_sem)
    keep.start()
    copies = []
    for number, peer in enumerate(far + across):
        copy = pltpu.make_async_remote_copy(
            src_ref=mine,
            dst_ref=out.at[slot],
            send_sem=send_sem.at[number],
            recv_sem=recv_sem.at[number],
            device_id=peer,
            device_id_type=MESH,
        )
        copy.start()
        copies.append(copy)
    keep.wait()
    for copy in copies:
        copy.wait()


def share_stats(stats):
    vmem = pl.BlockSpec(memory_space=pltpu.VMEM)
    return pl.pallas_call(
        share_kernel,
        out_shape=jax.ShapeDtypeStruct((NX * NK, NK, 8, ALLR), F32),
        in_specs=[vmem],
        out_specs=vmem,
        scratch_shapes=[
            pltpu.SemaphoreType.DMA((7,)),
            pltpu.SemaphoreType.DMA((7,)),
            pltpu.SemaphoreType.DMA(()),
        ],
        compiler_params=pltpu.CompilerParams(collective_id=1, has_side_effects=True),
        name="share_stats",
    )(stats)


def grads_kernel(
    sel_ref, keys_ref, q_ref, g_ref, stats_ref, dkeys_ref, dq_ref, landed, kbuf, dq_acc, spots, owns, sem
):
    z, y, core, x = where_am_i()
    chip = y * NZ + z

    def clear(i, carry):
        dkeys_ref[i] = jnp.zeros((ROWS, 128), BF16)
        return carry

    lax.fori_loop(0, NY * NZ, clear, 0)
    for qb in range(NK):
        count = list_slots(sel_ref, spots, owns, qb, 4 * core + x, (chip * NK + qb) * 4 + 3)
        chunks = (count + CHUNK - 1) // CHUNK

        @pl.when(chunks > 0)
        def _():
            load_chunk(0, spots, keys_ref, landed, kbuf, sem, 0)

        top = stats_ref[0, qb, 0:1, :]
        for d in range(1, NX * NK):
            top = jnp.maximum(top, stats_ref[d, qb, 0:1, :])
        total = jnp.zeros((1, ALLR), F32)
        delta = jnp.zeros((1, ALLR), F32)
        for d in range(NX * NK):
            shrink = jnp.exp(stats_ref[d, qb, 0:1, :] - top)
            total = total + shrink * stats_ref[d, qb, 1:2, :]
            delta = delta + shrink * stats_ref[d, qb, 2:3, :]
        inverse = 1.0 / total
        delta = delta * inverse
        dq_acc[...] = jnp.zeros((ALLR, WIDE), F32)

        def step(chunk, carry):
            slot = lax.rem(chunk, 2)

            @pl.when(chunk + 1 < chunks)
            def _():
                load_chunk(chunk + 1, spots, keys_ref, landed, kbuf, sem, 1 - slot)

            take_chunk(keys_ref, landed, kbuf, sem, slot)
            seen = seen_of(chunk, owns, count)
            scores = SCALE * nt(kbuf[...], q_ref[qb])
            dprobs = nt(kbuf[:, :VDIM], g_ref[qb])
            probs = jnp.where(seen, jnp.exp(jnp.where(seen, scores, NEG) - top), 0.0) * inverse
            probs16 = probs.astype(BF16)
            dscores16 = (probs * (dprobs - delta)).astype(BF16)
            dq_acc[...] += tn(dscores16, kbuf[...])
            dkeys = SCALE * nn(dscores16, q_ref[qb])
            dvalues = nn(probs16, g_ref[qb])
            front = dkeys[:, :VDIM] + dvalues
            back = dkeys[:, VDIM:]
            for i in range(CHUNK):
                slot_now = chunk * CHUNK + i

                @pl.when(slot_now < count)
                def _():
                    spot = spots[slot_now]
                    for g in range(4):
                        old = dkeys_ref[spot, 64 * g : 64 * g + 64, :].astype(F32)
                        new = front[64 * i : 64 * i + 64, 128 * g : 128 * g + 128]
                        dkeys_ref[spot, 64 * g : 64 * g + 64, :] = (old + new).astype(BF16)
                    old = dkeys_ref[spot, 256:288, :].astype(F32)
                    new = back[64 * i : 64 * i + 32] + pltpu.roll(back[64 * i + 32 : 64 * i + 64], 64, axis=1)
                    dkeys_ref[spot, 256:288, :] = (old + new).astype(BF16)

            return carry

        lax.fori_loop(0, chunks, step, 0)
        for g in range(NX):
            dq_ref[qb, g] = (SCALE * dq_acc[QR * g : QR * g + QR, :]).astype(BF16)


def grads_of(sel, keys, queries, grad_out, stats):
    vmem = pl.BlockSpec(memory_space=pltpu.VMEM)
    return pl.pallas_call(
        grads_kernel,
        out_shape=(
            jax.ShapeDtypeStruct((NY * NZ, ROWS, 128), BF16),
            jax.ShapeDtypeStruct((NK, NX, QR, WIDE), BF16),
        ),
        in_specs=[
            pl.BlockSpec(memory_space=pltpu.SMEM),
            pl.BlockSpec(memory_space=pl.ANY),
            vmem,
            vmem,
            vmem,
        ],
        out_specs=(vmem, vmem),
        scratch_shapes=[
            pltpu.VMEM((2, CHUNK, ROWS, 128), BF16),
            pltpu.VMEM((CK, WIDE), BF16),
            pltpu.VMEM((ALLR, WIDE), F32),
            pltpu.SMEM((SLOTS + CHUNK,), jnp.int32),
            pltpu.SMEM((SLOTS + CHUNK,), jnp.int32),
            pltpu.SemaphoreType.DMA((2, CHUNK)),
        ],
        compiler_params=pltpu.CompilerParams(vmem_limit_bytes=VMEM_LIMIT),
        name="local_grads",
    )(sel, keys, queries, grad_out, stats)


def return_kernel(
    dkeys_ref, dq_ref, dq_out, lat_out,
    got, tsum, total, quarters, dq_got, send_sem, recv_sem, qsend, qrecv, lsend, lrecv,
):
    z, y, core, x = where_am_i()
    far, across = group_peers(y, z, core, x)
    peers = far + across
    enter(ring_peers(y, z, core, x) + peers)
    first = {0: z, 1: y}
    second = {0: y, 1: z}
    sends = []

    def part(half):
        return pl.ds(HALF * half, HALF)

    def number(half, ring, way, left, q):
        return half * NLAB + LABELS[(ring, -way, left + 1, q)]

    def arrival(half, ring, way, left, q):
        at = number(half, ring, way, left, q)
        pltpu.make_async_copy(got.at[at], got.at[at], recv_sem.at[at]).wait()
        return at

    def local(half, off, along):
        spot = place(half, wrap(first[half] + off, RING), wrap(second[half] + along, RING))
        return dkeys_ref.at[spot, part(half)]

    def push(src, half, ring, way, left, q):
        at = number(half, ring, way, left, q)
        copy = pltpu.make_async_remote_copy(
            src_ref=src,
            dst_ref=got.at[at],
            send_sem=send_sem.at[at],
            recv_sem=recv_sem.at[at],
            device_id=neighbour(half, ring, way, y, z, core, x),
            device_id_type=MESH,
        )
        copy.start()
        sends.append(copy)

    def row_total(half, q):
        value = local(half, OFFS[q], 0)[...].astype(F32)
        for way in (1, -1):
            at = arrival(half, 1, way, 0, q)
            value = value + got[at].astype(F32)
        return value

    def send_row(half, q):
        off = OFFS[q]
        way, dist = (1, off) if off > 0 else (-1, -off)
        value = row_total(half, q)
        if (0, -way, dist + 1, 0) in LABELS:
            at = arrival(half, 0, way, dist, 0)
            value = value + got[at].astype(F32)
        tsum[half, q] = value.astype(BF16)
        push(tsum.at[half, q], half, 0, way, dist - 1, 0)

    def send_big(half, way, left, q):
        reach = UP[q] if way == -1 else DOWN[q]
        if left == reach - 1:
            push(local(half, OFFS[q], way * (left + 1)), half, 1, way, left, q)
        else:
            at = arrival(half, 1, way, left + 1, q)
            got[at] = (got[at].astype(F32) + local(half, OFFS[q], way * (left + 1))[...].astype(F32)).astype(BF16)
            push(got.at[at], half, 1, way, left, q)

    plan = gather_plan()
    waves = max(e[0] for e in plan) + 1
    for wave in reversed(range(waves)):
        for q, off in enumerate(OFFS):
            if off != 0 and abs(off) - 1 == wave:
                for half in (0, 1):
                    send_row(half, q)
        for entry_wave, ring, way, s, q in plan:
            if ring == 1 and entry_wave == wave:
                for half in (0, 1):
                    send_big(half, -way, s, q)
        if wave == waves - 2:
            for number_here, (ctx, head) in enumerate(peers):
                to_core = core if number_here < 3 else 1 - core
                copy = pltpu.make_async_remote_copy(
                    src_ref=dq_ref.at[to_core, head],
                    dst_ref=dq_got.at[number_here],
                    send_sem=qsend.at[number_here],
                    recv_sem=qrecv.at[number_here],
                    device_id=(ctx, head),
                    device_id_type=MESH,
                )
                copy.start()
                sends.append(copy)

    for half in (0, 1):
        value = row_total(half, 0)
        for way in (1, -1):
            at = arrival(half, 0, way, 0, 0)
            value = value + got[at].astype(F32)
        total[HALF * half : HALF * half + HALF, :] = value

    lane = lax.broadcasted_iota(jnp.int32, (32, 128), 1)
    tail = total[256:288, :]
    low = jnp.where(lane < 64, tail, 0.0)
    high = jnp.where(lane < 64, pltpu.roll(tail, 64, axis=1), 0.0)
    whole = jnp.concatenate(
        [total[64 * g : 64 * g + 64, :] for g in range(4)] + [jnp.concatenate([low, high], axis=0)], axis=1
    )
    for g in range(NX):
        share = LAT // NX
        turned = whole if g == 0 else pltpu.roll(whole, WIDE - share * g, axis=1)
        quarters[g] = turned[:, :share].astype(BF16)
    for d, peer in enumerate(far):
        copy = pltpu.make_async_remote_copy(
            src_ref=quarters.at[peer[1]],
            dst_ref=lat_out.at[x],
            send_sem=lsend.at[d],
            recv_sem=lrecv.at[d],
            device_id=peer,
            device_id_type=MESH,
        )
        copy.start()
        sends.append(copy)
    lat_out[x] = quarters[x]

    for number_here in range(7):
        pltpu.make_async_copy(
            dq_got.at[number_here], dq_got.at[number_here], qrecv.at[number_here]
        ).wait()
    for pair in range(HEADS_HERE // 2):
        rows = pl.ds(16 * pair, 16)
        value = dq_ref[core, x, rows, :].astype(F32)
        for number_here in range(7):
            value = value + dq_got[number_here, rows, :].astype(F32)
        one, two = value[:QBLK], pltpu.roll(value[QBLK:], 64, axis=1)
        dq_out[:, 2 * LAT * pair : 2 * LAT * (pair + 1)] = jnp.concatenate(
            [one[:, :VDIM], one[:, VDIM:] + two[:, :128], two[:, 128:]], axis=1
        ).astype(BF16)
    for d in range(3):
        pltpu.make_async_copy(lat_out.at[0], lat_out.at[0], lrecv.at[d]).wait()
    for copy in sends:
        copy.wait_send()


def return_all(dkeys, dq):
    vmem = pl.BlockSpec(memory_space=pltpu.VMEM)
    return pl.pallas_call(
        return_kernel,
        out_shape=(
            jax.ShapeDtypeStruct((QBLK, HEADS_HERE * LAT), BF16),
            jax.ShapeDtypeStruct((4, BLK, LAT // NX), BF16),
        ),
        in_specs=[vmem, vmem],
        out_specs=(vmem, vmem),
        scratch_shapes=[
            pltpu.VMEM((2 * NLAB, HALF, 128), BF16),
            pltpu.VMEM((2, len(OFFS), HALF, 128), BF16),
            pltpu.VMEM((ROWS, 128), F32),
            pltpu.VMEM((NX, BLK, LAT // NX), BF16),
            pltpu.VMEM((7, QR, WIDE), BF16),
            pltpu.SemaphoreType.DMA((2 * NLAB,)),
            pltpu.SemaphoreType.DMA((2 * NLAB,)),
            pltpu.SemaphoreType.DMA((7,)),
            pltpu.SemaphoreType.DMA((7,)),
            pltpu.SemaphoreType.DMA((3,)),
            pltpu.SemaphoreType.DMA((3,)),
        ],
        compiler_params=pltpu.CompilerParams(
            collective_id=2, has_side_effects=True, vmem_limit_bytes=VMEM_LIMIT
        ),
        cost_estimate=pl.CostEstimate(flops=0, bytes_accessed=10_000_000, transcendentals=0),
        name="return_grads",
    )(dkeys, dq)


def local(queries, grad_out, latent, selected):
    keys, all_q, all_g, sel = gather_all(latent, queries, grad_out, selected)
    all_q = all_q.reshape(NK, ALLR, WIDE)
    all_g = all_g.reshape(NK, ALLR, VDIM)
    stats = share_stats(stats_of(sel, keys, all_q, all_g))
    dkeys, dq = grads_of(sel, keys, all_q, all_g, stats)
    return return_all(dkeys, dq)


def solution(mesh):
    placed = (P("ctx", "head"), P("ctx", "head"), P("ctx", None, None), P("ctx", None))
    return jax.shard_map(
        local,
        mesh=mesh,
        in_specs=placed,
        out_specs=(P("ctx", "head"), P("ctx", None, "head")),
        check_vma=False,
    )
```

time: 427 us -> 144 us (0.34)
  the two profiles are of different devices: /device:TPU:1 before, /device:TPU:8 now
where the time goes in v1:
time: 144 us; the launch traced here: 143 us
  Pallas kernels  140 us (97%)
  local copies, waits for them, and re-layouts  3.15 us (2%)
    pallas_call x1, Pallas kernels, return_all(): pl.pallas_call(return_kernel, out_shape=(jax.ShapeDtypeStruct((QBLK, HEAD...  57.2 us
    pallas_call x1, Pallas kernels, gather_all(): pl.pallas_call(gather_kernel, out_shape=(jax.ShapeDtypeStruct((NY * NZ, R...  54.3 us
    pallas_call x1, Pallas kernels, grads_of(): pl.pallas_call(grads_kernel, out_shape=(jax.ShapeDtypeStruct((NY * NZ, RO...  11.5 us
    pallas_call x1, Pallas kernels, share_stats(): pl.pallas_call(share_kernel, out_shape=jax.ShapeDtypeStruct((NX * NK, NK,...  9.7 us
    pallas_call x1, Pallas kernels, stats_of(): pl.pallas_call(stats_kernel, out_shape=jax.ShapeDtypeStruct((NK, 8, ALLR)...  6.87 us
    unnamed x2, local copies, waits for them, and re-layouts  3.15 us

profile of v1, /device:TPU:8, one launch (start us, length us, event | category | flops | bytes accessed | tf_op | source)
XLA Modules:
  0.0 143.4 jit_solution(5778349174032615563)
XLA Ops:
  0.6 54.3 %gather_keys.1 = (bf16[64,288,128]{2,1,0:T(8,128)(2,1)}, bf16[2,4,128,640]{3,2,1,0:T(8,128)(2,1)}, bf16[2,4,128,512]{3,2,1,0:T(8,128)(2,1)}, s32[2,1,32]{2,1,0:T(1,128)}) custom-call(bf16[4,64,576]{2,1,0:T(8,128)(2,1)} %lat_ref.1, bf16[8,9216]{1,0:T(8,128)(2,1)} %q_ref.1, bf16[8,8192]{1,0:T(8,128)(2,1)} %g_ref.1, s32[1,32]{1,0:T(1,128)} %sel_ref.1), custom_call_target="tpu_custom_call" | custom-call | bytes 10000000 | tf_op jit(solution)/shard_map/gather_keys/pallas_call | solution.py:251
  54.9 6.9 %local_stats.1.mine = f32[2,8,512]{2,1,0:T(8,128)} custom-call(s32[2,1,32]{2,1,0:T(1,128)} %get-tuple-element.8.sel_ref, bf16[64,288,128]{2,1,0:T(8,128)(2,1)} %get-tuple-element.9.keys_ref, bf16[2,512,640]{2,1,0:T(8,128)(2,1)} %bitcast.2, bf16[2,512,512]{2,1,0:T(8,128)(2,1)} %bitcast.4), custom_call_target="tpu_custom_call" | custom-call | tf_op jit(solution)/shard_map/local_stats/pallas_call | solution.py:378
  61.8 9.7 %share_stats.1.stats_ref = f32[8,2,8,512]{3,2,1,0:T(8,128)} custom-call(f32[2,8,512]{2,1,0:T(8,128)} %local_stats.1.mine), custom_call_target="tpu_custom_call" | custom-call | tf_op jit(solution)/shard_map/share_stats/pallas_call | solution.py:426
  71.5 11.5 %local_grads.1 = (bf16[64,288,128]{2,1,0:T(8,128)(2,1)}, bf16[2,4,128,640]{3,2,1,0:T(8,128)(2,1)}) custom-call(s32[2,1,32]{2,1,0:T(1,128)} %get-tuple-element.8.sel_ref, bf16[64,288,128]{2,1,0:T(8,128)(2,1)} %get-tuple-element.9.keys_ref, bf16[2,512,640]{2,1,0:T(8,128)(2,1)} %bitcast.3, bf16[2,512,512]{2,1,0:T(8,128)(2,1)} %bitcast.5, ...), custom_call_target="tpu_custom_call" | custom-call | tf_op jit(solution)/shard_map/local_grads/pallas_call | solution.py:515
  83.0 57.2 %return_grads.1 = (bf16[8,9216]{1,0:T(8,128)(2,1)}, bf16[4,64,144]{2,1,0:T(8,128)(2,1)}) custom-call(bf16[64,288,128]{2,1,0:T(8,128)(2,1)} %get-tuple-element.12.dkeys_ref, bf16[2,4,128,640]{3,2,1,0:T(8,128)(2,1)} %get-tuple-element.13.dq_ref), custom_call_target="tpu_custom_call" | custom-call | bytes 10000000 | tf_op jit(solution)/shard_map/return_grads/pallas_call | solution.py:685
  140.3 1.6 %copy.8 = bf16[8,9216]{1,0:T(8,128)(2,1)} copy(bf16[8,9216]{1,0:T(8,128)(2,1)} %get-tuple-element.16) | data formatting | bytes 294912
  141.8 1.6 %copy.9 = bf16[4,64,144]{2,1,0:T(8,128)(2,1)} copy(bf16[4,64,144]{2,1,0:T(8,128)(2,1)} %get-tuple-element.17) | data formatting | bytes 147456

commit v2 on v1

--- a/solution.py
+++ b/solution.py
@@ -59,28 +59,94 @@
     return (ctx_of(wrap(y + step, NY), z, core), x)
 
 
+READY, WORK = 15.0, 0.5
+PASS = ((6.0, (0, 3)), (6.2, (1, 1)), (9.0, (1, 3)), (9.2, (0, 1)), (12.0, (0, 2)), (12.2, (1, 2)))
+PIECE, DELAY = 0.72, 1.5
+
+
 def gather_plan():
-    plan = []
-    for t in range(4):
-        plan.append((t, 0, 1, t, 0))
-        if t < 3:
-            plan.append((t, 0, -1, t, 0))
-    for q, off in enumerate(OFFS):
-        for s in range(UP[q]):
-            plan.append((s + abs(off), 1, 1, s, q))
-        for s in range(DOWN[q]):
-            plan.append((s + abs(off), 1, -1, s, q))
-    return sorted(plan, key=lambda e: (e[0], e[1], -e[3], e[4], -e[2]))
+    sends = {}
+    for half in (0, 1):
+        for t in range(4):
+            sends[(half, 0, 1, t, 0)] = (half, 0, 1, t - 1, 0) if t else None
+        for t in range(3):
+            sends[(half, 0, -1, t, 0)] = (half, 0, -1, t - 1, 0) if t else None
+        for q, off in enumerate(OFFS):
+            root = (half, 0, 1 if off < 0 else -1, abs(off) - 1, 0) if off else None
+            for s in range(UP[q]):
+                sends[(half, 1, 1, s, q)] = (half, 1, 1, s - 1, q) if s else root
+            for s in range(DOWN[q]):
+                sends[(half, 1, -1, s, q)] = (half, 1, -1, s - 1, q) if s else root
+    left = {}
+    for key in sends:
+        length, at = 0, key
+        while at is not None:
+            left[at] = max(left.get(at, 0), length)
+            length, at = length + 1, sends[at]
+    free, ready, order = {}, {k: 0.0 for k in sends if sends[k] is None}, []
+
+    def link(key):
+        return (key[0] ^ key[1], key[2])
+
+    while ready:
+        at = min(ready, key=lambda k: (round(max(ready[k], free.get(link(k), 0.0)), 3), -left[k], k))
+        since = ready.pop(at)
+        begin = max(since, free.get(link(at), 0.0))
+        free[link(at)] = begin + PIECE
+        order.append((begin, since, at))
+        for key, root in sends.items():
+            if root == at:
+                ready[key] = begin + PIECE + DELAY
+    return order
 
 
 def labels():
     names = {}
-    for wave, ring, way, s, q in gather_plan():
-        names[(ring, way, s + 1, q)] = len(names)
+    for begin, since, (half, ring, way, s, q) in gather_plan():
+        if half == 0:
+            names[(ring, way, s + 1, q)] = len(names)
     return names
 
 
 LABELS = labels()
+
+
+def route(half, dy, dz):
+    off, along = (dz, dy) if half == 0 else (dy, dz)
+    if along == 0:
+        return None if off == 0 else (0, 1 if off < 0 else -1, abs(off), 0)
+    q = OFFS.index(off)
+    if along == -4 and UP[q] < 4:
+        return (1, -1, 4, q)
+    return (1, 1 if along < 0 else -1, abs(along), q)
+
+
+def gather_steps():
+    lands = {(None, 0): 0.0, (None, 1): 0.0}
+    for begin, since, (half, ring, way, s, q) in gather_plan():
+        lands[((ring, way, s + 1, q), half)] = begin + PIECE + DELAY
+    blocks = []
+    for dy in OFFS:
+        for dz in OFFS:
+            blocks.append((max(lands[(route(half, dy, dz), half)] for half in (0, 1)), dy, dz))
+    blocks.sort(key=lambda b: (b[0], abs(b[1]) + abs(b[2]), b))
+    work, clock = [], READY
+    for first in range(0, len(blocks), CHUNK):
+        group = blocks[first : first + CHUNK]
+        clock = max(clock, group[-1][0] * 1.15 + 0.5)
+        for qb in range(NK):
+            work.append((clock, qb, [b[1:] for b in group]))
+            clock = clock + WORK
+    sends = gather_plan()
+    merged = []
+    marks = [(1.0, "start")] + [(t, "pass") + what for t, what in PASS] + [(t, "work", qb, group) for t, qb, group in work]
+    marks.sort(key=lambda m: m[0])
+    for mark in marks:
+        for entry in [e for e in sends if e[1] * 1.15 + 0.5 <= mark[0] or mark[1] in ('start', 'pass') and e[1] <= mark[0]]:
+            merged.append(("send", entry[2]))
+            sends.remove(entry)
+        merged.append(mark[1:])
+    return merged + [("send", entry[2]) for entry in sends]
 NLAB = len(LABELS)
 
 
@@ -110,15 +176,16 @@
 
 def gather_kernel(
     lat_ref, q_ref, g_ref, sel_ref,
-    keys_out, q_out, g_out, sel_out,
-    block, pack, qrow, grow, load_sem, local_sem, send_sem, recv_sem, gsend, grecv,
+    keys_final, q_final, g_final, sel_final, stats_all,
+    keys_out, q_out, g_out, sel_out, block, pack, qrow, grow, stats, unseen,
+    load_sem, local_sem, out_sem, send_sem, recv_sem, gsend, grecv, ssend, srecv,
 ):
     z, y, core, x = where_am_i()
     chip = y * NZ + z
     load = pltpu.make_async_copy(lat_ref.at[x], block, load_sem)
     load.start()
     far, across = group_peers(y, z, core, x)
-    enter(ring_peers(y, z, core, x) + far + across[:1])
+    enter(ring_peers(y, z, core, x) + far + across)
     load.wait()
     wide = block[...].astype(F32)
     for g in range(4):
@@ -171,9 +238,6 @@
         copy.start()
         sends.append(copy)
 
-    plan = gather_plan()
-    waves = max(e[0] for e in plan) + 1
-
     def group_copy(src, out, kind, slot_core, slot_x, peer, number):
         copy = pltpu.make_async_remote_copy(
             src_ref=src,
@@ -195,54 +259,139 @@
         ref = (q_out.at[0, 0], g_out.at[0, 0], sel_out.at[0])[kind]
         pltpu.make_async_copy(ref, ref, grecv.at[number_of(kind, hop)]).wait()
 
-    for wave in range(waves):
-        for entry in plan:
-            if entry[0] == wave:
-                for half in (0, 1):
-                    send(half, *entry[1:])
-        if wave == 0:
-            group_copy(sel_ref, sel_out, 2, core, 0, across[0], number_of(2, 0))
-            keep_sel = pltpu.make_async_copy(sel_ref, sel_out.at[core], local_sem.at[1])
-            keep_sel.start()
-            for pair in range(HEADS_HERE // 2):
-                both = q_ref[:, 2 * LAT * pair : 2 * LAT * (pair + 1)].astype(F32)
-                lane = lax.broadcasted_iota(jnp.int32, (QBLK, WIDE), 1)
-                one = jnp.where(lane < LAT, both[:, :WIDE], 0.0)
-                two = jnp.where(lane < LAT, pltpu.roll(both[:, VDIM:], WIDE - 64, axis=1), 0.0)
-                qrow[16 * pair : 16 * pair + 16, :] = jnp.concatenate([one, two], axis=0).astype(BF16)
-                one = g_ref[:, 2 * VDIM * pair : 2 * VDIM * pair + VDIM].astype(F32)
-                two = g_ref[:, 2 * VDIM * pair + VDIM : 2 * VDIM * (pair + 1)].astype(F32)
-                grow[16 * pair : 16 * pair + 16, :] = jnp.concatenate([one, two], axis=0).astype(BF16)
-            for d in range(3):
-                group_copy(qrow, q_out, 0, core, x, far[d], number_of(0, 3 - d))
-                group_copy(grow, g_out, 1, core, x, far[d], number_of(1, 3 - d))
-            group_copy(qrow, q_out, 0, core, x, across[0], number_of(0, 4))
-            group_copy(grow, g_out, 1, core, x, across[0], number_of(1, 4))
-            keep_q = pltpu.make_async_copy(qrow, q_out.at[core, x], local_sem.at[2])
-            keep_q.start()
-            keep_g = pltpu.make_async_copy(grow, g_out.at[core, x], local_sem.at[3])
-            keep_g.start()
-        if wave == 5:
-            for d in (1, 3, 2):
-                src_x = wrap(x + d, NX)
-                group_arrival(0, d)
-                group_copy(q_out.at[core, src_x], q_out, 0, core, src_x, across[0], number_of(0, 4 + d))
-                group_arrival(1, d)
-                group_copy(g_out.at[core, src_x], g_out, 1, core, src_x, across[0], number_of(1, 4 + d))
-
-    for half in (0, 1):
-        for label in LABELS:
-            arrival(half, label)
-    for kind in (0, 1):
-        for hop in (4, 5, 6, 7):
-            group_arrival(kind, hop)
-    group_arrival(2, 0)
+    def start_group():
+        group_copy(sel_ref, sel_out, 2, core, 0, across[0], number_of(2, 0))
+        keep_sel.start()
+        for pair in range(HEADS_HERE // 2):
+            both = q_ref[:, 2 * LAT * pair : 2 * LAT * (pair + 1)].astype(F32)
+            lane = lax.broadcasted_iota(jnp.int32, (QBLK, WIDE), 1)
+            one = jnp.where(lane < LAT, both[:, :WIDE], 0.0)
+            two = jnp.where(lane < LAT, pltpu.roll(both[:, VDIM:], WIDE - 64, axis=1), 0.0)
+            qrow[16 * pair : 16 * pair + 16, :] = jnp.concatenate([one, two], axis=0).astype(BF16)
+            one = g_ref[:, 2 * VDIM * pair : 2 * VDIM * pair + VDIM].astype(F32)
+            two = g_ref[:, 2 * VDIM * pair + VDIM : 2 * VDIM * (pair + 1)].astype(F32)
+            grow[16 * pair : 16 * pair + 16, :] = jnp.concatenate([one, two], axis=0).astype(BF16)
+        group_copy(qrow, q_out, 0, core, x, far[0], number_of(0, 3))
+        group_copy(grow, g_out, 1, core, x, far[2], number_of(1, 1))
+        group_copy(qrow, q_out, 0, core, x, across[0], number_of(0, 4))
+        group_copy(grow, g_out, 1, core, x, across[0], number_of(1, 4))
+        group_copy(grow, g_out, 1, core, x, far[0], number_of(1, 3))
+        group_copy(qrow, q_out, 0, core, x, far[2], number_of(0, 1))
+        keep_q.start()
+        keep_g.start()
+
+    def pass_on(kind, hop):
+        src_x = wrap(x + hop, NX)
+        group_arrival(kind, hop)
+        out = (q_out, g_out)[kind]
+        if (kind, hop) == (0, 3):
+            group_copy(out.at[core, src_x], out, kind, core, src_x, far[0], number_of(kind, 2))
+        if (kind, hop) == (1, 1):
+            group_copy(out.at[core, src_x], out, kind, core, src_x, far[2], number_of(kind, 2))
+        group_copy(out.at[core, src_x], out, kind, core, src_x, across[0], number_of(kind, 4 + hop))
+
+    keep_sel = pltpu.make_async_copy(sel_ref, sel_out.at[core], local_sem.at[1])
+    keep_q = pltpu.make_async_copy(qrow, q_out.at[core, x], local_sem.at[2])
+    keep_g = pltpu.make_async_copy(grow, g_out.at[core, x], local_sem.at[3])
+    finals = [
+        pltpu.make_async_copy(q_out, q_final, local_sem.at[4]),
+        pltpu.make_async_copy(g_out, g_final, local_sem.at[5]),
+        pltpu.make_async_copy(sel_out, sel_final, local_sem.at[6]),
+    ]
+
+    def group_done():
+        for kind in (0, 1):
+            for hop in (4, 5, 6, 7):
+                group_arrival(kind, hop)
+        group_arrival(2, 0)
+        keep_sel.wait()
+        keep_q.wait()
+        keep_g.wait()
+        for copy in finals:
+            copy.start()
+        ids = lax.broadcasted_iota(jnp.int32, (NY * NZ, SLOTS), 0) * 8 + 4 * core + x
+        for qb in range(NK):
+            hit = jnp.max(jnp.where(sel_out[qb] == ids, 1.0, 0.0), axis=1, keepdims=True)
+            unseen[qb] = jnp.broadcast_to(jnp.where(hit > 0.0, 0.0, NEG), (NY * NZ, 128))
+            stats[3 * qb : 3 * qb + 3, :] = jnp.concatenate(
+                [jnp.full((1, ALLR), NEG, F32), jnp.zeros((2, ALLR), F32)], axis=0
+            )
+
+    lane = lax.broadcasted_iota(jnp.int32, (32, 128), 1)
+
+    def work(qb, group):
+        fronts, tails, hides = [], [], []
+        for dy, dz in group:
+            for half in (0, 1):
+                label = route(half, dy, dz)
+                if label is not None:
+                    arrival(half, label)
+            spot = wrap(y + dy, NY) * NZ + wrap(z + dz, NZ)
+            if (dy, dz) == (0, 0) and qb == 0:
+                keep.wait()
+            if qb == 0:
+                pltpu.make_async_copy(keys_out.at[spot], keys_final.at[spot], out_sem).start()
+            fronts.append(jnp.concatenate([keys_out[spot, 64 * g : 64 * g + 64, :] for g in range(4)], axis=1))
+            tail = keys_out[spot, 256:288, :].astype(F32)
+            low = jnp.where(lane < 64, tail, 0.0)
+            high = jnp.where(lane < 64, pltpu.roll(tail, 64, axis=1), 0.0)
+            tails.append(jnp.concatenate([low, high], axis=0).astype(BF16))
+            hide = jnp.concatenate([unseen[qb, pl.ds(spot, 1), :]] * 4, axis=1)
+            hide = jnp.broadcast_to(hide, (BLK, ALLR))
+            if (dy, dz) == (0, 0):
+                row = lax.broadcasted_iota(jnp.int32, (BLK, ALLR), 0)
+                col = lax.broadcasted_iota(jnp.int32, (BLK, ALLR), 1)
+                late = row > BLK - QBLK + lax.rem(col, QBLK)
+                own = (x == NX - 1) & (core == qb)
+                hide = jnp.where(late & own, NEG, hide)
+            hides.append(hide)
+        front = jnp.concatenate(fronts, axis=0)
+        whole = jnp.concatenate([front, jnp.concatenate(tails, axis=0)], axis=1)
+        scores = SCALE * nt(whole, q_out[qb].reshape(ALLR, WIDE)) + jnp.concatenate(hides, axis=0)
+        dprobs = nt(front, g_out[qb].reshape(ALLR, VDIM))
+        top = stats[3 * qb : 3 * qb + 1, :]
+        new_top = jnp.maximum(top, jnp.max(scores, axis=0, keepdims=True))
+        weights = jnp.exp(scores - new_top)
+        shrink = jnp.exp(top - new_top)
+        total = stats[3 * qb + 1 : 3 * qb + 2, :] * shrink + jnp.sum(weights, axis=0, keepdims=True)
+        delta = stats[3 * qb + 2 : 3 * qb + 3, :] * shrink + jnp.sum(weights * dprobs, axis=0, keepdims=True)
+        stats[3 * qb : 3 * qb + 3, :] = jnp.concatenate([new_top, total, delta], axis=0)
+
+    stats[...] = jnp.zeros((8, ALLR), F32)
+    begun = False
+    for mark in gather_steps():
+        if mark[0] == "send":
+            send(*mark[1])
+        elif mark[0] == "start":
+            start_group()
+        elif mark[0] == "pass":
+            pass_on(*mark[1:])
+        else:
+            if not begun:
+                group_done()
+                begun = True
+            work(*mark[1:])
+
+    slot = x * NK + core
+    for number, peer in enumerate(far + across):
+        copy = pltpu.make_async_remote_copy(
+            src_ref=stats,
+            dst_ref=stats_all.at[slot],
+            send_sem=ssend.at[number],
+            recv_sem=srecv.at[number],
+            device_id=peer,
+            device_id_type=MESH,
+        )
+        copy.start()
+        sends.append(copy)
+    stats_all[slot] = stats[...]
+    for number in range(7):
+        pltpu.make_async_copy(stats_all.at[0], stats_all.at[0], srecv.at[number]).wait()
     for copy in sends:
         copy.wait_send()
-    keep.wait()
-    keep_sel.wait()
-    keep_q.wait()
-    keep_g.wait()
+    for copy in finals:
+        copy.wait()
+    pltpu.make_async_copy(keys_out, keys_final, out_sem).wait()
 
 
 def gather_all(latent, queries, grad_out, selected):
@@ -255,20 +404,30 @@
             jax.ShapeDtypeStruct((NK, NX, QR, WIDE), BF16),
             jax.ShapeDtypeStruct((NK, NX, QR, VDIM), BF16),
             jax.ShapeDtypeStruct((NK, 1, SLOTS), jnp.int32),
+            jax.ShapeDtypeStruct((NX * NK, 8, ALLR), F32),
         ),
         in_specs=[any_spec, vmem, vmem, any_spec],
-        out_specs=(any_spec, any_spec, any_spec, any_spec),
+        out_specs=(any_spec, any_spec, any_spec, any_spec, vmem),
         scratch_shapes=[
+            pltpu.VMEM((NY * NZ, ROWS, 128), BF16),
+            pltpu.VMEM((NK, NX, QR, WIDE), BF16),
+            pltpu.VMEM((NK, NX, QR, VDIM), BF16),
+            pltpu.VMEM((NK, 1, SLOTS), jnp.int32),
             pltpu.VMEM((BLK, LAT), BF16),
             pltpu.VMEM((ROWS, 128), BF16),
             pltpu.VMEM((QR, WIDE), BF16),
             pltpu.VMEM((QR, VDIM), BF16),
+            pltpu.VMEM((8, ALLR), F32),
+            pltpu.VMEM((NK, NY * NZ, 128), F32),
             pltpu.SemaphoreType.DMA(()),
-            pltpu.SemaphoreType.DMA((4,)),
+            pltpu.SemaphoreType.DMA((7,)),
+            pltpu.SemaphoreType.DMA(()),
             pltpu.SemaphoreType.DMA((2 * NLAB,)),
             pltpu.SemaphoreType.DMA((2 * NLAB,)),
             pltpu.SemaphoreType.DMA((15,)),
             pltpu.SemaphoreType.DMA((15,)),
+            pltpu.SemaphoreType.DMA((7,)),
+            pltpu.SemaphoreType.DMA((7,)),
         ],
         compiler_params=pltpu.CompilerParams(
             collective_id=0, has_side_effects=True, vmem_limit_bytes=VMEM_LIMIT
@@ -337,107 +496,6 @@
     return lax.dot_general(a, b, (((1,), (0,)), ((), ())), preferred_element_type=F32)
 
 
-def stats_kernel(sel_ref, keys_ref, q_ref, g_ref, stats_ref, landed, kbuf, spots, owns, sem):
-    z, y, core, x = where_am_i()
-    chip = y * NZ + z
-    for qb in range(NK):
-        count = list_slots(sel_ref, spots, owns, qb, 4 * core + x, (chip * NK + qb) * 4 + 3)
-        chunks = (count + CHUNK - 1) // CHUNK
-
-        @pl.when(chunks > 0)
-        def _():
-            load_chunk(0, spots, keys_ref, landed, kbuf, sem, 0)
-
-        def step(chunk, carry):
-            top, total, delta = carry
-            slot = lax.rem(chunk, 2)
-
-            @pl.when(chunk + 1 < chunks)
-            def _():
-                load_chunk(chunk + 1, spots, keys_ref, landed, kbuf, sem, 1 - slot)
-
-            take_chunk(keys_ref, landed, kbuf, sem, slot)
-            seen = seen_of(chunk, owns, count)
-            scores = SCALE * nt(kbuf[...], q_ref[qb])
-            dprobs = nt(kbuf[:, :VDIM], g_ref[qb])
-            scores = jnp.where(seen, scores, NEG)
-            new_top = jnp.maximum(top, jnp.max(scores, axis=0, keepdims=True))
-            weights = jnp.where(seen, jnp.exp(scores - new_top), 0.0)
-            shrink = jnp.exp(top - new_top)
-            total = total * shrink + jnp.sum(weights, axis=0, keepdims=True)
-            delta = delta * shrink + jnp.sum(weights * dprobs, axis=0, keepdims=True)
-            return new_top, total, delta
-
-        zero = jnp.zeros((1, ALLR), F32)
-        top, total, delta = lax.fori_loop(0, chunks, step, (zero + NEG, zero, zero))
-        stats_ref[qb] = jnp.concatenate([top, total, delta, jnp.zeros((5, ALLR), F32)], axis=0)
-
-
-def stats_of(sel, keys, queries, grad_out):
-    vmem = pl.BlockSpec(memory_space=pltpu.VMEM)
-    return pl.pallas_call(
-        stats_kernel,
-        out_shape=jax.ShapeDtypeStruct((NK, 8, ALLR), F32),
-        in_specs=[
-            pl.BlockSpec(memory_space=pltpu.SMEM),
-            pl.BlockSpec(memory_space=pl.ANY),
-            vmem,
-            vmem,
-        ],
-        out_specs=vmem,
-        scratch_shapes=[
-            pltpu.VMEM((2, CHUNK, ROWS, 128), BF16),
-            pltpu.VMEM((CK, WIDE), BF16),
-            pltpu.SMEM((SLOTS + CHUNK,), jnp.int32),
-            pltpu.SMEM((SLOTS + CHUNK,), jnp.int32),
-            pltpu.SemaphoreType.DMA((2, CHUNK)),
-        ],
-        compiler_params=pltpu.CompilerParams(vmem_limit_bytes=VMEM_LIMIT),
-        name="local_stats",
-    )(sel, keys, queries, grad_out)
-
-
-def share_kernel(mine, out, send_sem, recv_sem, local_sem):
-    z, y, core, x = where_am_i()
-    far, across = group_peers(y, z, core, x)
-    enter(far + across)
-    slot = x * NK + core
-    keep = pltpu.make_async_copy(mine, out.at[slot], local_sem)
-    keep.start()
-    copies = []
-    for number, peer in enumerate(far + across):
-        copy = pltpu.make_async_remote_copy(
-            src_ref=mine,
-            dst_ref=out.at[slot],
-            send_sem=send_sem.at[number],
-            recv_sem=recv_sem.at[number],
-            device_id=peer,
-            device_id_type=MESH,
-        )
-        copy.start()
-        copies.append(copy)
-    keep.wait()
-    for copy in copies:
-        copy.wait()
-
-
-def share_stats(stats):
-    vmem = pl.BlockSpec(memory_space=pltpu.VMEM)
-    return pl.pallas_call(
-        share_kernel,
-        out_shape=jax.ShapeDtypeStruct((NX * NK, NK, 8, ALLR), F32),
-        in_specs=[vmem],
-        out_specs=vmem,
-        scratch_shapes=[
-            pltpu.SemaphoreType.DMA((7,)),
-            pltpu.SemaphoreType.DMA((7,)),
-            pltpu.SemaphoreType.DMA(()),
-        ],
-        compiler_params=pltpu.CompilerParams(collective_id=1, has_side_effects=True),
-        name="share_stats",
-    )(stats)
-
-
 def grads_kernel(
     sel_ref, keys_ref, q_ref, g_ref, stats_ref, dkeys_ref, dq_ref, landed, kbuf, dq_acc, spots, owns, sem
 ):
@@ -457,15 +515,15 @@
         def _():
             load_chunk(0, spots, keys_ref, landed, kbuf, sem, 0)
 
-        top = stats_ref[0, qb, 0:1, :]
+        top = stats_ref[0, 3 * qb : 3 * qb + 1, :]
         for d in range(1, NX * NK):
-            top = jnp.maximum(top, stats_ref[d, qb, 0:1, :])
+            top = jnp.maximum(top, stats_ref[d, 3 * qb : 3 * qb + 1, :])
         total = jnp.zeros((1, ALLR), F32)
         delta = jnp.zeros((1, ALLR), F32)
         for d in range(NX * NK):
-            shrink = jnp.exp(stats_ref[d, qb, 0:1, :] - top)
-            total = total + shrink * stats_ref[d, qb, 1:2, :]
-            delta = delta + shrink * stats_ref[d, qb, 2:3, :]
+            shrink = jnp.exp(stats_ref[d, 3 * qb : 3 * qb + 1, :] - top)
+            total = total + shrink * stats_ref[d, 3 * qb + 1 : 3 * qb + 2, :]
+            delta = delta + shrink * stats_ref[d, 3 * qb + 2 : 3 * qb + 3, :]
         inverse = 1.0 / total
         delta = delta * inverse
         dq_acc[...] = jnp.zeros((ALLR, WIDE), F32)
@@ -605,18 +663,12 @@
             got[at] = (got[at].astype(F32) + local(half, OFFS[q], way * (left + 1))[...].astype(F32)).astype(BF16)
             push(got.at[at], half, 1, way, left, q)
 
-    plan = gather_plan()
-    waves = max(e[0] for e in plan) + 1
-    for wave in reversed(range(waves)):
-        for q, off in enumerate(OFFS):
-            if off != 0 and abs(off) - 1 == wave:
-                for half in (0, 1):
-                    send_row(half, q)
-        for entry_wave, ring, way, s, q in plan:
-            if ring == 1 and entry_wave == wave:
-                for half in (0, 1):
-                    send_big(half, -way, s, q)
-        if wave == waves - 2:
+    for turn, (begin, since, (half, ring, way, s, q)) in enumerate(reversed(gather_plan())):
+        if ring == 0:
+            send_row(half, OFFS.index(-way * (s + 1)))
+        else:
+            send_big(half, -way, s, q)
+        if turn == 24:
             for number_here, (ctx, head) in enumerate(peers):
                 to_core = core if number_here < 3 else 1 - core
                 copy = pltpu.make_async_remote_copy(
@@ -712,10 +764,9 @@
 
 
 def local(queries, grad_out, latent, selected):
-    keys, all_q, all_g, sel = gather_all(latent, queries, grad_out, selected)
+    keys, all_q, all_g, sel, stats = gather_all(latent, queries, grad_out, selected)
     all_q = all_q.reshape(NK, ALLR, WIDE)
     all_g = all_g.reshape(NK, ALLR, VDIM)
-    stats = share_stats(stats_of(sel, keys, all_q, all_g))
     dkeys, dq = grads_of(sel, keys, all_q, all_g, stats)
     return return_all(dkeys, dq)
 

time: 144 us -> 120 us (0.83)
  Pallas kernels: 140 us -> 116 us
    pallas_call x2 -> x0, Pallas kernels: 16.6 us -> none  [the longest x1 9.7 us: share_stats(): pl.pallas_call(share_kernel, out_shape=jax.ShapeDtypeStruct((NX * NK, NK,...]
    pallas_call x1, Pallas kernels: 57.2 us -> 47.8 us  [return_all(): pl.pallas_call(return_kernel, out_shape=(jax.ShapeDtypeStruct((QBLK, HEAD...]
    pallas_call x1, Pallas kernels: 54.3 us -> 57 us  [gather_all(): pl.pallas_call(gather_kernel, out_shape=(jax.ShapeDtypeStruct((NY * NZ, R...]
where the time goes in v2:
time: 120 us; the launch traced here: 119 us
  Pallas kernels  116 us (97%)
  local copies, waits for them, and re-layouts  3.15 us (3%)
    pallas_call x1, Pallas kernels, gather_all(): pl.pallas_call(gather_kernel, out_shape=(jax.ShapeDtypeStruct((NY * NZ, R...  57 us
    pallas_call x1, Pallas kernels, return_all(): pl.pallas_call(return_kernel, out_shape=(jax.ShapeDtypeStruct((QBLK, HEAD...  47.8 us
    pallas_call x1, Pallas kernels, grads_of(): pl.pallas_call(grads_kernel, out_shape=(jax.ShapeDtypeStruct((NY * NZ, RO...  10.8 us
    unnamed x2, local copies, waits for them, and re-layouts  3.15 us

profile of v2, /device:TPU:8, one launch (start us, length us, event | category | flops | bytes accessed | tf_op | source)
XLA Modules:
  0.0 119.4 jit_solution(17843848153604773857)
XLA Ops:
  0.6 57.0 %gather_keys.1 = (bf16[64,288,128]{2,1,0:T(8,128)(2,1)}, bf16[2,4,128,640]{3,2,1,0:T(8,128)(2,1)}, bf16[2,4,128,512]{3,2,1,0:T(8,128)(2,1)}, s32[2,1,32]{2,1,0:T(1,128)}, f32[8,8,512]{2,1,0:T(8,128)}) custom-call(bf16[4,64,576]{2,1,0:T(8,128)(2,1)} %lat_ref.1, bf16[8,9216]{1,0:T(8,128)(2,1)} %q_ref.1, bf16[8,8192]{1,0:T(8,128)(2,1)} %g_ref.1, s32[1,32]{1,0:T(1,128)} %sel_ref.1), custom_call_target="tpu_custom_call" | custom-call | bytes 10000000 | tf_op jit(solution)/shard_map/gather_keys/pallas_call | solution.py:400
  57.6 10.8 %local_grads.1 = (bf16[64,288,128]{2,1,0:T(8,128)(2,1)}, bf16[2,4,128,640]{3,2,1,0:T(8,128)(2,1)}) custom-call(s32[2,1,32]{2,1,0:T(1,128)} %get-tuple-element.9.sel_ref, bf16[64,288,128]{2,1,0:T(8,128)(2,1)} %get-tuple-element.10.keys_ref, bf16[2,512,640]{2,1,0:T(8,128)(2,1)} %bitcast.2, bf16[2,512,512]{2,1,0:T(8,128)(2,1)} %bitcast.3, ...), custom_call_target="tpu_custom_call" | custom-call | tf_op jit(solution)/shard_map/local_grads/pallas_call | solution.py:573
  68.4 47.8 %return_grads.1 = (bf16[8,9216]{1,0:T(8,128)(2,1)}, bf16[4,64,144]{2,1,0:T(8,128)(2,1)}) custom-call(bf16[64,288,128]{2,1,0:T(8,128)(2,1)} %get-tuple-element.14.dkeys_ref, bf16[2,4,128,640]{3,2,1,0:T(8,128)(2,1)} %get-tuple-element.15.dq_ref), custom_call_target="tpu_custom_call" | custom-call | bytes 10000000 | tf_op jit(solution)/shard_map/return_grads/pallas_call | solution.py:737
  116.2 1.6 %copy.8 = bf16[8,9216]{1,0:T(8,128)(2,1)} copy(bf16[8,9216]{1,0:T(8,128)(2,1)} %get-tuple-element.18) | data formatting | bytes 294912
  117.8 1.6 %copy.9 = bf16[4,64,144]{2,1,0:T(8,128)(2,1)} copy(bf16[4,64,144]{2,1,0:T(8,128)(2,1)} %get-tuple-element.19) | data formatting | bytes 147456

commit v3 on v2

--- a/solution.py
+++ b/solution.py
@@ -23,9 +23,10 @@
 ALLR = QR * NX
 SLOTS = 32
 CHUNK = 4
+GROUP = 4
 CK = CHUNK * BLK
 NEG = -1e30
-VMEM_LIMIT = 56 * 1024 * 1024
+VMEM_LIMIT = 24 * 1024 * 1024
 
 OFFS = (0, -1, 1, -2, 2, -3, 3, -4)
 UP = (4, 4, 4, 4, 3, 3, 3, 3)
@@ -131,15 +132,14 @@
             blocks.append((max(lands[(route(half, dy, dz), half)] for half in (0, 1)), dy, dz))
     blocks.sort(key=lambda b: (b[0], abs(b[1]) + abs(b[2]), b))
     work, clock = [], READY
-    for first in range(0, len(blocks), CHUNK):
-        group = blocks[first : first + CHUNK]
+    for first in range(0, len(blocks), GROUP):
+        group = blocks[first : first + GROUP]
         clock = max(clock, group[-1][0] * 1.15 + 0.5)
-        for qb in range(NK):
-            work.append((clock, qb, [b[1:] for b in group]))
-            clock = clock + WORK
+        work.append((clock, [b[1:] for b in group]))
+        clock = clock + 2 * WORK
     sends = gather_plan()
     merged = []
-    marks = [(1.0, "start")] + [(t, "pass") + what for t, what in PASS] + [(t, "work", qb, group) for t, qb, group in work]
+    marks = [(1.0, "start")] + [(t, "pass") + what for t, what in PASS] + [(t, "work", group) for t, group in work]
     marks.sort(key=lambda m: m[0])
     for mark in marks:
         for entry in [e for e in sends if e[1] * 1.15 + 0.5 <= mark[0] or mark[1] in ('start', 'pass') and e[1] <= mark[0]]:
@@ -175,15 +175,19 @@
 
 
 def gather_kernel(
-    lat_ref, q_ref, g_ref, sel_ref,
-    keys_final, q_final, g_final, sel_final, stats_all,
-    keys_out, q_out, g_out, sel_out, block, pack, qrow, grow, stats, unseen,
-    load_sem, local_sem, out_sem, send_sem, recv_sem, gsend, grecv, ssend, srecv,
+    lat_ref, q_hbm, g_hbm, sel_ref,
+    keys_out, q_out, g_out, sel_out, stats_all,
+    block, pack, q_ref, g_ref, qrow, grow, stats, unseen,
+    load_sem, local_sem, send_sem, recv_sem, gsend, grecv, ssend, srecv,
 ):
     z, y, core, x = where_am_i()
     chip = y * NZ + z
     load = pltpu.make_async_copy(lat_ref.at[x], block, load_sem)
     load.start()
+    load_q = pltpu.make_async_copy(q_hbm, q_ref, local_sem.at[4])
+    load_q.start()
+    load_g = pltpu.make_async_copy(g_hbm, g_ref, local_sem.at[5])
+    load_g.start()
     far, across = group_peers(y, z, core, x)
     enter(ring_peers(y, z, core, x) + far + across)
     load.wait()
@@ -262,6 +266,8 @@
     def start_group():
         group_copy(sel_ref, sel_out, 2, core, 0, across[0], number_of(2, 0))
         keep_sel.start()
+        load_q.wait()
+        load_g.wait()
         for pair in range(HEADS_HERE // 2):
             both = q_ref[:, 2 * LAT * pair : 2 * LAT * (pair + 1)].astype(F32)
             lane = lax.broadcasted_iota(jnp.int32, (QBLK, WIDE), 1)
@@ -293,12 +299,6 @@
     keep_sel = pltpu.make_async_copy(sel_ref, sel_out.at[core], local_sem.at[1])
     keep_q = pltpu.make_async_copy(qrow, q_out.at[core, x], local_sem.at[2])
     keep_g = pltpu.make_async_copy(grow, g_out.at[core, x], local_sem.at[3])
-    finals = [
-        pltpu.make_async_copy(q_out, q_final, local_sem.at[4]),
-        pltpu.make_async_copy(g_out, g_final, local_sem.at[5]),
-        pltpu.make_async_copy(sel_out, sel_final, local_sem.at[6]),
-    ]
-
     def group_done():
         for kind in (0, 1):
             for hop in (4, 5, 6, 7):
@@ -307,8 +307,6 @@
         keep_sel.wait()
         keep_q.wait()
         keep_g.wait()
-        for copy in finals:
-            copy.start()
         ids = lax.broadcasted_iota(jnp.int32, (NY * NZ, SLOTS), 0) * 8 + 4 * core + x
         for qb in range(NK):
             hit = jnp.max(jnp.where(sel_out[qb] == ids, 1.0, 0.0), axis=1, keepdims=True)
@@ -319,43 +317,44 @@
 
     lane = lax.broadcasted_iota(jnp.int32, (32, 128), 1)
 
-    def work(qb, group):
-        fronts, tails, hides = [], [], []
+    def work(group):
+        fronts, tails, hides = [], [], [[], []]
         for dy, dz in group:
             for half in (0, 1):
                 label = route(half, dy, dz)
                 if label is not None:
                     arrival(half, label)
             spot = wrap(y + dy, NY) * NZ + wrap(z + dz, NZ)
-            if (dy, dz) == (0, 0) and qb == 0:
+            if (dy, dz) == (0, 0):
                 keep.wait()
-            if qb == 0:
-                pltpu.make_async_copy(keys_out.at[spot], keys_final.at[spot], out_sem).start()
             fronts.append(jnp.concatenate([keys_out[spot, 64 * g : 64 * g + 64, :] for g in range(4)], axis=1))
             tail = keys_out[spot, 256:288, :].astype(F32)
             low = jnp.where(lane < 64, tail, 0.0)
             high = jnp.where(lane < 64, pltpu.roll(tail, 64, axis=1), 0.0)
             tails.append(jnp.concatenate([low, high], axis=0).astype(BF16))
-            hide = jnp.concatenate([unseen[qb, pl.ds(spot, 1), :]] * 4, axis=1)
-            hide = jnp.broadcast_to(hide, (BLK, ALLR))
-            if (dy, dz) == (0, 0):
-                row = lax.broadcasted_iota(jnp.int32, (BLK, ALLR), 0)
-                col = lax.broadcasted_iota(jnp.int32, (BLK, ALLR), 1)
-                late = row > BLK - QBLK + lax.rem(col, QBLK)
-                own = (x == NX - 1) & (core == qb)
-                hide = jnp.where(late & own, NEG, hide)
-            hides.append(hide)
+            for qb in range(NK):
+                hide = jnp.concatenate([unseen[qb, pl.ds(spot, 1), :]] * 4, axis=1)
+                hide = jnp.broadcast_to(hide, (BLK, ALLR))
+                if (dy, dz) == (0, 0):
+                    row = lax.broadcasted_iota(jnp.int32, (BLK, ALLR), 0)
+                    col = lax.broadcasted_iota(jnp.int32, (BLK, ALLR), 1)
+                    late = row > BLK - QBLK + lax.rem(col, QBLK)
+                    own = (x == NX - 1) & (core == qb)
+                    hide = jnp.where(late & own, NEG, hide)
+                hides[qb].append(hide)
         front = jnp.concatenate(fronts, axis=0)
         whole = jnp.concatenate([front, jnp.concatenate(tails, axis=0)], axis=1)
-        scores = SCALE * nt(whole, q_out[qb].reshape(ALLR, WIDE)) + jnp.concatenate(hides, axis=0)
-        dprobs = nt(front, g_out[qb].reshape(ALLR, VDIM))
-        top = stats[3 * qb : 3 * qb + 1, :]
-        new_top = jnp.maximum(top, jnp.max(scores, axis=0, keepdims=True))
-        weights = jnp.exp(scores - new_top)
-        shrink = jnp.exp(top - new_top)
-        total = stats[3 * qb + 1 : 3 * qb + 2, :] * shrink + jnp.sum(weights, axis=0, keepdims=True)
-        delta = stats[3 * qb + 2 : 3 * qb + 3, :] * shrink + jnp.sum(weights * dprobs, axis=0, keepdims=True)
-        stats[3 * qb : 3 * qb + 3, :] = jnp.concatenate([new_top, total, delta], axis=0)
+        scores = [nt(whole, q_out[qb].reshape(ALLR, WIDE)) for qb in range(NK)]
+        dprobs = [nt(front, g_out[qb].reshape(ALLR, VDIM)) for qb in range(NK)]
+        for qb in range(NK):
+            score = SCALE * scores[qb] + jnp.concatenate(hides[qb], axis=0)
+            top = stats[3 * qb : 3 * qb + 1, :]
+            new_top = jnp.maximum(top, jnp.max(score, axis=0, keepdims=True))
+            weights = jnp.exp(score - new_top)
+            shrink = jnp.exp(top - new_top)
+            total = stats[3 * qb + 1 : 3 * qb + 2, :] * shrink + jnp.sum(weights, axis=0, keepdims=True)
+            delta = stats[3 * qb + 2 : 3 * qb + 3, :] * shrink + jnp.sum(weights * dprobs[qb], axis=0, keepdims=True)
+            stats[3 * qb : 3 * qb + 3, :] = jnp.concatenate([new_top, total, delta], axis=0)
 
     stats[...] = jnp.zeros((8, ALLR), F32)
     begun = False
@@ -389,13 +388,10 @@
         pltpu.make_async_copy(stats_all.at[0], stats_all.at[0], srecv.at[number]).wait()
     for copy in sends:
         copy.wait_send()
-    for copy in finals:
-        copy.wait()
-    pltpu.make_async_copy(keys_out, keys_final, out_sem).wait()
 
 
 def gather_all(latent, queries, grad_out, selected):
-    any_spec = pl.BlockSpec(memory_space=pl.ANY)
+    hbm = pl.BlockSpec(memory_space=pltpu.HBM)
     vmem = pl.BlockSpec(memory_space=pltpu.VMEM)
     return pl.pallas_call(
         gather_kernel,
@@ -406,22 +402,19 @@
             jax.ShapeDtypeStruct((NK, 1, SLOTS), jnp.int32),
             jax.ShapeDtypeStruct((NX * NK, 8, ALLR), F32),
         ),
-        in_specs=[any_spec, vmem, vmem, any_spec],
-        out_specs=(any_spec, any_spec, any_spec, any_spec, vmem),
+        in_specs=[hbm] * 4,
+        out_specs=(vmem,) * 5,
         scratch_shapes=[
-            pltpu.VMEM((NY * NZ, ROWS, 128), BF16),
-            pltpu.VMEM((NK, NX, QR, WIDE), BF16),
-            pltpu.VMEM((NK, NX, QR, VDIM), BF16),
-            pltpu.VMEM((NK, 1, SLOTS), jnp.int32),
             pltpu.VMEM((BLK, LAT), BF16),
             pltpu.VMEM((ROWS, 128), BF16),
+            pltpu.VMEM((QBLK, HEADS_HERE * LAT), BF16),
+            pltpu.VMEM((QBLK, HEADS_HERE * VDIM), BF16),
             pltpu.VMEM((QR, WIDE), BF16),
             pltpu.VMEM((QR, VDIM), BF16),
             pltpu.VMEM((8, ALLR), F32),
             pltpu.VMEM((NK, NY * NZ, 128), F32),
             pltpu.SemaphoreType.DMA(()),
-            pltpu.SemaphoreType.DMA((7,)),
-            pltpu.SemaphoreType.DMA(()),
+            pltpu.SemaphoreType.DMA((6,)),
             pltpu.SemaphoreType.DMA((2 * NLAB,)),
             pltpu.SemaphoreType.DMA((2 * NLAB,)),
             pltpu.SemaphoreType.DMA((15,)),
@@ -434,7 +427,7 @@
         ),
         cost_estimate=pl.CostEstimate(flops=0, bytes_accessed=10_000_000, transcendentals=0),
         name="gather_keys",
-    )(latent, queries, grad_out, selected)
+    )(*[pltpu.with_memory_space_constraint(a, pltpu.HBM) for a in (latent, queries, grad_out, selected)])
 
 
 def list_slots(sel_ref, spots, owns, query_block, kind, own_id):
@@ -452,20 +445,13 @@
     return count
 
 
-def load_chunk(chunk, spots, keys_ref, landed, kbuf, sem, slot):
-    for i in range(CHUNK):
-        pltpu.make_async_copy(
-            keys_ref.at[spots[chunk * CHUNK + i]], landed.at[slot, i], sem.at[slot, i]
-        ).start()
-
-
-def take_chunk(keys_ref, landed, kbuf, sem, slot):
+def take_chunk(chunk, spots, keys_ref, kbuf):
     lane = lax.broadcasted_iota(jnp.int32, (32, 128), 1)
     for i in range(CHUNK):
-        pltpu.make_async_copy(keys_ref.at[0], landed.at[slot, i], sem.at[slot, i]).wait()
+        spot = spots[chunk * CHUNK + i]
         for g in range(4):
-            kbuf[64 * i : 64 * i + 64, 128 * g : 128 * g + 128] = landed[slot, i, 64 * g : 64 * g + 64, :]
-        tail = landed[slot, i, 256:288, :].astype(F32)
+            kbuf[64 * i : 64 * i + 64, 128 * g : 128 * g + 128] = keys_ref[spot, 64 * g : 64 * g + 64, :]
+        tail = keys_ref[spot, 256:288, :].astype(F32)
         kbuf[64 * i : 64 * i + 32, VDIM:] = jnp.where(lane < 64, tail, 0.0).astype(BF16)
         kbuf[64 * i + 32 : 64 * i + 64, VDIM:] = jnp.where(
             lane < 64, pltpu.roll(tail, 64, axis=1), 0.0
@@ -497,7 +483,7 @@
 
 
 def grads_kernel(
-    sel_ref, keys_ref, q_ref, g_ref, stats_ref, dkeys_ref, dq_ref, landed, kbuf, dq_acc, spots, owns, sem
+    sel_ref, keys_ref, q_ref, g_ref, stats_ref, dkeys_ref, dq_ref, kbuf, dq_acc, spots, owns
 ):
     z, y, core, x = where_am_i()
     chip = y * NZ + z
@@ -510,10 +496,6 @@
     for qb in range(NK):
         count = list_slots(sel_ref, spots, owns, qb, 4 * core + x, (chip * NK + qb) * 4 + 3)
         chunks = (count + CHUNK - 1) // CHUNK
-
-        @pl.when(chunks > 0)
-        def _():
-            load_chunk(0, spots, keys_ref, landed, kbuf, sem, 0)
 
         top = stats_ref[0, 3 * qb : 3 * qb + 1, :]
         for d in range(1, NX * NK):
@@ -529,13 +511,7 @@
         dq_acc[...] = jnp.zeros((ALLR, WIDE), F32)
 
         def step(chunk, carry):
-            slot = lax.rem(chunk, 2)
-
-            @pl.when(chunk + 1 < chunks)
-            def _():
-                load_chunk(chunk + 1, spots, keys_ref, landed, kbuf, sem, 1 - slot)
-
-            take_chunk(keys_ref, landed, kbuf, sem, slot)
+            take_chunk(chunk, spots, keys_ref, kbuf)
             seen = seen_of(chunk, owns, count)
             scores = SCALE * nt(kbuf[...], q_ref[qb])
             dprobs = nt(kbuf[:, :VDIM], g_ref[qb])
@@ -578,19 +554,17 @@
         ),
         in_specs=[
             pl.BlockSpec(memory_space=pltpu.SMEM),
-            pl.BlockSpec(memory_space=pl.ANY),
+            vmem,
             vmem,
             vmem,
             vmem,
         ],
         out_specs=(vmem, vmem),
         scratch_shapes=[
-            pltpu.VMEM((2, CHUNK, ROWS, 128), BF16),
             pltpu.VMEM((CK, WIDE), BF16),
             pltpu.VMEM((ALLR, WIDE), F32),
             pltpu.SMEM((SLOTS + CHUNK,), jnp.int32),
             pltpu.SMEM((SLOTS + CHUNK,), jnp.int32),
-            pltpu.SemaphoreType.DMA((2, CHUNK)),
         ],
         compiler_params=pltpu.CompilerParams(vmem_limit_bytes=VMEM_LIMIT),
         name="local_grads",

time: 120 us -> 105 us (0.88)
  Pallas kernels: 116 us -> 103 us
  local copies, waits for them, and re-layouts: 3.15 us -> 1.32 us
    pallas_call x1, Pallas kernels: 10.8 us -> 4.21 us  [grads_of(): pl.pallas_call(grads_kernel, out_shape=(jax.ShapeDtypeStruct((NY * NZ, RO...]
    pallas_call x1, Pallas kernels: 47.8 us -> 44.3 us  [return_all(): pl.pallas_call(return_kernel, out_shape=(jax.ShapeDtypeStruct((QBLK, HEAD...]
    pallas_call x1, Pallas kernels: 57 us -> 54.8 us  [gather_all(): pl.pallas_call(gather_kernel, out_shape=(jax.ShapeDtypeStruct((NY * NZ, R...]
    unnamed x2, local copies, waits for them, and re-layouts: 3.15 us -> 1.32 us
where the time goes in v3:
time: 105 us
  Pallas kernels  103 us (98%)
  local copies, waits for them, and re-layouts  1.32 us (1%)
    pallas_call x1, Pallas kernels, gather_all(): pl.pallas_call(gather_kernel, out_shape=(jax.ShapeDtypeStruct((NY * NZ, R...  54.8 us
    pallas_call x1, Pallas kernels, return_all(): pl.pallas_call(return_kernel, out_shape=(jax.ShapeDtypeStruct((QBLK, HEAD...  44.3 us
    pallas_call x1, Pallas kernels, grads_of(): pl.pallas_call(grads_kernel, out_shape=(jax.ShapeDtypeStruct((NY * NZ, RO...  4.21 us

profile of v3, /device:TPU:8, one launch (start us, length us, event | category | flops | bytes accessed | tf_op | source)
XLA Modules:
  0.0 105.3 jit_solution(2810176980833861338)
XLA Ops:
  0.6 54.8 %gather_keys.1 = (bf16[64,288,128]{2,1,0:T(8,128)(2,1)S(1)}, bf16[2,4,128,640]{3,2,1,0:T(8,128)(2,1)S(1)}, bf16[2,4,128,512]{3,2,1,0:T(8,128)(2,1)S(1)}, s32[2,1,32]{2,1,0:T(1,128)S(1)}, f32[8,8,512]{2,1,0:T(8,128)S(1)}) custom-call(bf16[4,64,576]{2,1,0:T(8,128)(2,1)} %lat_ref.1, bf16[8,9216]{1,0:T(8,128)(2,1)} %q_hbm.1, bf16[8,8192]{1,0:T(8,128)(2,1)} %g_hbm.1, ...), custom_call_target="tpu_custom_call" | custom-call | bytes 10000000 | tf_op jit(solution)/shard_map/gather_keys/pallas_call | solution.py:396
  55.4 4.2 %local_grads.1 = (bf16[64,288,128]{2,1,0:T(8,128)(2,1)S(1)}, bf16[2,4,128,640]{3,2,1,0:T(8,128)(2,1)S(1)}) custom-call(s32[2,1,32]{2,1,0:T(1,128)S(1)} %get-tuple-element.9.sel_ref, bf16[64,288,128]{2,1,0:T(8,128)(2,1)S(1)} %get-tuple-element.10.keys_ref, bf16[2,512,640]{2,1,0:T(8,128)(2,1)S(1)} %bitcast.2, bf16[2,512,512]{2,1,0:T(8,128)(2,1)S(1)} %bitcast.3, ...), custom_call_target="tpu_custom_call" | custom-call | tf_op jit(solution)/shard_map/local_grads/pallas_call | solution.py:549
  59.7 44.3 %return_grads.1 = (bf16[8,9216]{1,0:T(8,128)(2,1)S(1)}, bf16[4,64,144]{2,1,0:T(8,128)(2,1)S(1)}) custom-call(bf16[64,288,128]{2,1,0:T(8,128)(2,1)S(1)} %get-tuple-element.14.dkeys_ref, bf16[2,4,128,640]{3,2,1,0:T(8,128)(2,1)S(1)} %get-tuple-element.15.dq_ref), custom_call_target="tpu_custom_call" | custom-call | bytes 10000000 | tf_op jit(solution)/shard_map/return_grads/pallas_call | solution.py:711
  104.0 0.7 copy.8
  104.6 0.7 copy.9

commit v4 on v3

--- a/solution.py
+++ b/solution.py
@@ -60,7 +60,7 @@
     return (ctx_of(wrap(y + step, NY), z, core), x)
 
 
-READY, WORK = 15.0, 0.5
+READY, WORK = 14.0, 0.5
 PASS = ((6.0, (0, 3)), (6.2, (1, 1)), (9.0, (1, 3)), (9.2, (0, 1)), (12.0, (0, 2)), (12.2, (1, 2)))
 PIECE, DELAY = 0.72, 1.5
 
@@ -139,7 +139,7 @@
         clock = clock + 2 * WORK
     sends = gather_plan()
     merged = []
-    marks = [(1.0, "start")] + [(t, "pass") + what for t, what in PASS] + [(t, "work", group) for t, group in work]
+    marks = [(0.5, "start")] + [(t, "pass") + what for t, what in PASS] + [(t, "work", group) for t, group in work]
     marks.sort(key=lambda m: m[0])
     for mark in marks:
         for entry in [e for e in sends if e[1] * 1.15 + 0.5 <= mark[0] or mark[1] in ('start', 'pass') and e[1] <= mark[0]]:
@@ -150,10 +150,12 @@
 NLAB = len(LABELS)
 
 
-def enter(peers):
+def enter(peers, meanwhile=None):
     barrier = pltpu.get_barrier_semaphore()
     for peer in peers:
         pl.semaphore_signal(barrier, inc=1, device_id=peer, device_id_type=MESH)
+    if meanwhile is not None:
+        meanwhile()
     pl.semaphore_wait(barrier, len(peers))
 
 
@@ -189,13 +191,26 @@
     load_g = pltpu.make_async_copy(g_hbm, g_ref, local_sem.at[5])
     load_g.start()
     far, across = group_peers(y, z, core, x)
-    enter(ring_peers(y, z, core, x) + far + across)
-    load.wait()
-    wide = block[...].astype(F32)
-    for g in range(4):
-        pack[64 * g : 64 * g + 64, :] = block[:, 128 * g : 128 * g + 128]
-    tail = jnp.concatenate([wide[:, VDIM:], jnp.zeros((BLK, 64), F32)], axis=1)
-    pack[256:288, :] = (tail[:32] + pltpu.roll(tail[32:], 64, axis=1)).astype(BF16)
+    def prepare():
+        load.wait()
+        wide = block[...].astype(F32)
+        for g in range(4):
+            pack[64 * g : 64 * g + 64, :] = block[:, 128 * g : 128 * g + 128]
+        tail = jnp.concatenate([wide[:, VDIM:], jnp.zeros((BLK, 64), F32)], axis=1)
+        pack[256:288, :] = (tail[:32] + pltpu.roll(tail[32:], 64, axis=1)).astype(BF16)
+        load_q.wait()
+        load_g.wait()
+        for pair in range(HEADS_HERE // 2):
+            both = q_ref[:, 2 * LAT * pair : 2 * LAT * (pair + 1)].astype(F32)
+            lane = lax.broadcasted_iota(jnp.int32, (QBLK, WIDE), 1)
+            one = jnp.where(lane < LAT, both[:, :WIDE], 0.0)
+            two = jnp.where(lane < LAT, pltpu.roll(both[:, VDIM:], WIDE - 64, axis=1), 0.0)
+            qrow[16 * pair : 16 * pair + 16, :] = jnp.concatenate([one, two], axis=0).astype(BF16)
+            one = g_ref[:, 2 * VDIM * pair : 2 * VDIM * pair + VDIM].astype(F32)
+            two = g_ref[:, 2 * VDIM * pair + VDIM : 2 * VDIM * (pair + 1)].astype(F32)
+            grow[16 * pair : 16 * pair + 16, :] = jnp.concatenate([one, two], axis=0).astype(BF16)
+
+    enter(ring_peers(y, z, core, x) + far + across, prepare)
     keep = pltpu.make_async_copy(pack, keys_out.at[chip], local_sem.at[0])
     keep.start()
 
@@ -266,17 +281,6 @@
     def start_group():
         group_copy(sel_ref, sel_out, 2, core, 0, across[0], number_of(2, 0))
         keep_sel.start()
-        load_q.wait()
-        load_g.wait()
-        for pair in range(HEADS_HERE // 2):
-            both = q_ref[:, 2 * LAT * pair : 2 * LAT * (pair + 1)].astype(F32)
-            lane = lax.broadcasted_iota(jnp.int32, (QBLK, WIDE), 1)
-            one = jnp.where(lane < LAT, both[:, :WIDE], 0.0)
-            two = jnp.where(lane < LAT, pltpu.roll(both[:, VDIM:], WIDE - 64, axis=1), 0.0)
-            qrow[16 * pair : 16 * pair + 16, :] = jnp.concatenate([one, two], axis=0).astype(BF16)
-            one = g_ref[:, 2 * VDIM * pair : 2 * VDIM * pair + VDIM].astype(F32)
-            two = g_ref[:, 2 * VDIM * pair + VDIM : 2 * VDIM * (pair + 1)].astype(F32)
-            grow[16 * pair : 16 * pair + 16, :] = jnp.concatenate([one, two], axis=0).astype(BF16)
         group_copy(qrow, q_out, 0, core, x, far[0], number_of(0, 3))
         group_copy(grow, g_out, 1, core, x, far[2], number_of(1, 1))
         group_copy(qrow, q_out, 0, core, x, across[0], number_of(0, 4))
@@ -515,7 +519,7 @@
             seen = seen_of(chunk, owns, count)
             scores = SCALE * nt(kbuf[...], q_ref[qb])
             dprobs = nt(kbuf[:, :VDIM], g_ref[qb])
-            probs = jnp.where(seen, jnp.exp(jnp.where(seen, scores, NEG) - top), 0.0) * inverse
+            probs = jnp.exp(jnp.where(seen, scores, NEG) - top) * inverse
             probs16 = probs.astype(BF16)
             dscores16 = (probs * (dprobs - delta)).astype(BF16)
             dq_acc[...] += tn(dscores16, kbuf[...])

time: 105 us -> 106 us (level)
  the two profiles are of different devices: /device:TPU:8 before, /device:TPU:16 now
where the time goes in v4:
time: 106 us; the launch traced here: 105 us
  Pallas kernels  103 us (97%)
  local copies, waits for them, and re-layouts  1.32 us (1%)
    pallas_call x1, Pallas kernels, gather_all(): pl.pallas_call(gather_kernel, out_shape=(jax.ShapeDtypeStruct((NY * NZ, R...  54.8 us
    pallas_call x1, Pallas kernels, return_all(): pl.pallas_call(return_kernel, out_shape=(jax.ShapeDtypeStruct((QBLK, HEAD...  41.4 us
    pallas_call x1, Pallas kernels, grads_of(): pl.pallas_call(grads_kernel, out_shape=(jax.ShapeDtypeStruct((NY * NZ, RO...  7.24 us

profile of v4, /device:TPU:16, one launch (start us, length us, event | category | flops | bytes accessed | tf_op | source)
XLA Modules:
  0.0 105.4 jit_solution(12468957954251717726)
XLA Ops:
  0.6 54.8 %gather_keys.1 = (bf16[64,288,128]{2,1,0:T(8,128)(2,1)S(1)}, bf16[2,4,128,640]{3,2,1,0:T(8,128)(2,1)S(1)}, bf16[2,4,128,512]{3,2,1,0:T(8,128)(2,1)S(1)}, s32[2,1,32]{2,1,0:T(1,128)S(1)}, f32[8,8,512]{2,1,0:T(8,128)S(1)}) custom-call(bf16[4,64,576]{2,1,0:T(8,128)(2,1)} %lat_ref.1, bf16[8,9216]{1,0:T(8,128)(2,1)} %q_hbm.1, bf16[8,8192]{1,0:T(8,128)(2,1)} %g_hbm.1, ...), custom_call_target="tpu_custom_call" | custom-call | bytes 10000000 | tf_op jit(solution)/shard_map/gather_keys/pallas_call | solution.py:400
  55.4 7.2 %local_grads.1 = (bf16[64,288,128]{2,1,0:T(8,128)(2,1)S(1)}, bf16[2,4,128,640]{3,2,1,0:T(8,128)(2,1)S(1)}) custom-call(s32[2,1,32]{2,1,0:T(1,128)S(1)} %get-tuple-element.9.sel_ref, bf16[64,288,128]{2,1,0:T(8,128)(2,1)S(1)} %get-tuple-element.10.keys_ref, bf16[2,512,640]{2,1,0:T(8,128)(2,1)S(1)} %bitcast.2, bf16[2,512,512]{2,1,0:T(8,128)(2,1)S(1)} %bitcast.3, ...), custom_call_target="tpu_custom_call" | custom-call | tf_op jit(solution)/shard_map/local_grads/pallas_call | solution.py:553
  62.7 41.4 %return_grads.1 = (bf16[8,9216]{1,0:T(8,128)(2,1)S(1)}, bf16[4,64,144]{2,1,0:T(8,128)(2,1)S(1)}) custom-call(bf16[64,288,128]{2,1,0:T(8,128)(2,1)S(1)} %get-tuple-element.14.dkeys_ref, bf16[2,4,128,640]{3,2,1,0:T(8,128)(2,1)S(1)} %get-tuple-element.15.dq_ref), custom_call_target="tpu_custom_call" | custom-call | bytes 10000000 | tf_op jit(solution)/shard_map/return_grads/pallas_call | solution.py:715
  104.1 0.7 copy.8
  104.8 0.7 copy.9
